TPU v7x, 256 devices: a whole 4x4x8 slice. The times are simulated.
256 devices in a mesh: row: 32 (over z, y), col: 8 (over x, core).
Axes of the slice: x: 4, y: 4, z: 8, core: 2. Of those that a mesh axis runs over, the one named last changes fastest.
Arguments:
- image: bfloat16 [16384, 512], P(('row', 'col')), may hold values from -2 to 2
- text: bfloat16 [16384, 512], P(('row', 'col')), may hold values from -3 to 3
- logit_scale: float32 [1], replicated, may hold values from 10 to 100
Outputs:
- loss: float32 [1], replicated
- grad_image: float32 [16384, 512], P(('row', 'col'))
- grad_text: float32 [16384, 512], P(('row', 'col'))
All inputs are finite; a program needn't handle non-finite values.
Results may differ from a plain program's by a relative error of at most 0.0095.
Values may be sent and summed in bfloat16 or wider, within the bound.
A program may use at most 64 MiB of HBM per device.

v0:
```python
import jax
import jax.numpy as jnp
from jax import lax
from jax.sharding import Mesh
from jax.sharding import PartitionSpec as P

COL = ("col_0", "col_1")
ROW = ("row_0", "row_1")
ROW_COL = ("row_0", "row_1", "col_0", "col_1")


def in_order(tiles, dim):
    tiles = jnp.moveaxis(tiles, 0, dim)
    dims = tiles.shape
    return tiles.reshape(*dims[:dim], dims[dim] * dims[dim + 1], *dims[dim + 2 :])


def from_everyone(value, axis):
    copies = jnp.broadcast_to(value, (lax.axis_size(axis), *value.shape))
    return lax.all_to_all(copies, axis, split_axis=0, concat_axis=0, tiled=True)


def gathered_copies(value, axis, dim):
    return in_order(from_everyone(value, axis), dim)


def gather_axes(value, axes, dim):
    for axis in reversed(axes):
        value = lax.all_gather(value, axis, axis=dim, tiled=True)
    return value


def all_in_one(value, axis):
    leaves = jax.tree.leaves(value)
    turns = sorted(range(len(leaves)), key=lambda k: -leaves[k].size)
    width = (1, *leaves[turns[0]].shape)[-1]
    lines = [
        jnp.pad(leaves[k].reshape(-1), (0, -leaves[k].size % width)).reshape(-1, width)
        for k in turns
    ]
    both, at, found = (from_everyone(jnp.concatenate(lines), axis), 0, {})
    for k, line in zip(turns, lines):
        share = both[:, at : at + len(line)].reshape(len(both), -1)
        found[k] = share[:, : leaves[k].size].reshape(-1, *leaves[k].shape)
        at += len(line)
    numbers = iter(range(len(leaves)))
    return jax.tree.map(lambda _: found[next(numbers)], value)


def joined_by_halves(pieces, combine):
    while len(jax.tree.leaves(pieces)[0]) > 1:
        pieces = jax.vmap(combine)(
            *(jax.tree.map(lambda part: part[side::2], pieces) for side in (0, 1))
        )
    return jax.tree.map(lambda part: part[0], pieces)


def combined_all(value, axis, combine):
    pieces = all_in_one(value, axis)
    return joined_by_halves(pieces, combine)


def all_in_one_2(value, axis):
    leaves = jax.tree.leaves(value)
    turns = sorted(range(len(leaves)), key=lambda k: -leaves[k].size)
    width = (1, *leaves[turns[0]].shape)[-1]
    lines = [
        jnp.pad(leaves[k].reshape(-1), (0, -leaves[k].size % width)).reshape(-1, width)
        for k in turns
    ]
    both, at, found = (lax.all_gather(jnp.concatenate(lines), axis), 0, {})
    for k, line in zip(turns, lines):
        share = both[:, at : at + len(line)].reshape(len(both), -1)
        found[k] = share[:, : leaves[k].size].reshape(-1, *leaves[k].shape)
        at += len(line)
    numbers = iter(range(len(leaves)))
    return jax.tree.map(lambda _: found[next(numbers)], value)


def merged_by_axis(value, axes, combine):
    for axis in axes:
        pieces = all_in_one_2(value, axis)
        value = jax.tree.map(lambda part: part[0], pieces)
        for k in range(1, lax.axis_size(axis)):
            value = combine(value, jax.tree.map(lambda part: part[k], pieces))
    return value


def over_axes(value, axes):
    for axis in axes:
        value = lax.psum(value, axis)
    return value


def sum_by_axis(total, axes):
    for axis in axes:
        total = lax.psum_scatter(total, axis, scatter_dimension=0, tiled=True)
    return total


def in_blocks(value, dim, count):
    dims = value.shape
    tiles = value.reshape(*dims[:dim], count, dims[dim] // count, *dims[dim + 1 :])
    return jnp.moveaxis(tiles, dim, 0)


def summed_on_arrival(value, axis, dim):
    count = lax.axis_size(axis)
    tiles = lax.all_to_all(in_blocks(value, dim, count), axis, 0, 0, tiled=True)
    return jnp.sum(tiles, axis=0)


def normalize(embedding):
    values = embedding.astype(jnp.float32)
    length = jnp.sqrt(jnp.sum(values * values, axis=1, keepdims=True) + 1e-06)
    return (values / length, length)


def unnormalize(unit_rows, length, gradient):
    return (gradient - unit_rows * jnp.sum(unit_rows * gradient, axis=1, keepdims=True)) / length


def combine(former, latter):
    summit = jnp.maximum(former[0], latter[0])
    return (
        summit,
        former[1] * jnp.exp(former[0] - summit) + latter[1] * jnp.exp(latter[0] - summit),
    )


def on_device(image, text, logit_scale):
    sharpness = logit_scale[0]
    unit_image, image_len = normalize(image)
    unit_text, text_len = normalize(text)
    img_own = unit_image.astype(jnp.bfloat16)
    txt_own = unit_text.astype(jnp.bfloat16)
    img_tile = gathered_copies(img_own, COL, 0)
    txt_tile = gather_axes(txt_own, ROW, 0)
    columns = txt_tile.shape[0]
    block_cols = min(512, columns)
    block_count = columns // block_cols
    txt_blocks = txt_tile.reshape(block_count, block_cols, txt_tile.shape[1])

    def scores(txt_block):
        return sharpness * jnp.einsum(
            "re,ce->rc", img_tile, txt_block, preferred_element_type=jnp.float32
        )

    lowest = jnp.full((img_tile.shape[0],), -1e30, jnp.float32)

    def online(running, txt_block):
        row_peak, row_sum = running
        logits = scores(txt_block)
        col_peak = jnp.max(logits, axis=0)
        col_sum = jnp.sum(jnp.exp(logits - col_peak[None, :]), axis=0)
        higher = jnp.maximum(row_peak, jnp.max(logits, axis=1))
        row_sum = row_sum * jnp.exp(row_peak - higher) + jnp.sum(
            jnp.exp(logits - higher[:, None]), axis=1
        )
        return ((higher, row_sum), (col_peak, col_sum))

    (row_peak, row_sum), (col_peak, col_sum) = lax.scan(
        online, (lowest, jnp.zeros_like(lowest)), txt_blocks
    )
    row_peak, row_sum = combined_all((row_peak, row_sum), COL, combine)
    col_peak, col_sum = merged_by_axis((col_peak.reshape(-1), col_sum.reshape(-1)), ROW, combine)
    row_lse = row_peak + jnp.log(row_sum)
    col_lse = col_peak + jnp.log(col_sum)
    own_rows = image.shape[0]
    row_mine = lax.dynamic_slice_in_dim(row_lse, lax.axis_index(COL) * own_rows, own_rows)
    col_mine = lax.dynamic_slice_in_dim(col_lse, lax.axis_index(ROW) * own_rows, own_rows)
    img_wide = img_own.astype(jnp.float32)
    txt_wide = txt_own.astype(jnp.float32)
    positive = sharpness * jnp.sum(img_wide * txt_wide, axis=1)
    partial_value = jnp.sum(row_mine - positive) + jnp.sum(col_mine - positive)
    overall = over_axes(partial_value, ROW_COL)
    batch_size = own_rows * lax.axis_size(ROW) * lax.axis_size(COL)
    loss = (overall / (2 * batch_size)).reshape(1)

    def weights_of(txt_block, lse_cols):
        logits = scores(txt_block)
        return (
            0.5 * (jnp.exp(logits - row_lse[:, None]) + jnp.exp(logits - lse_cols[None, :]))
        ).astype(jnp.bfloat16)

    start_grad = jnp.zeros((img_tile.shape[0], img_tile.shape[1]), jnp.float32)
    lse_blocks = col_lse.reshape(block_count, block_cols)

    def keep_weights(running, inputs):
        txt_block, lse_cols = inputs
        weights = weights_of(txt_block, lse_cols)
        running = running + sharpness * jnp.dot(
            weights, txt_block, preferred_element_type=jnp.float32
        )
        return (running, weights)

    img_terms, stored = lax.scan(keep_weights, start_grad, (txt_blocks, lse_blocks))
    flipped = jnp.swapaxes(stored, 1, 2).reshape(columns, img_tile.shape[0])
    txt_grad = sum_by_axis(
        sharpness * jnp.dot(flipped, img_tile, preferred_element_type=jnp.float32), ROW
    )
    img_grad = summed_on_arrival(img_terms, COL, 0)
    img_grad = img_grad - sharpness * txt_wide
    txt_grad = txt_grad - sharpness * img_wide
    return (
        loss,
        unnormalize(unit_image, image_len, img_grad),
        unnormalize(unit_text, text_len, txt_grad),
    )


def solution(mesh):
    torus = Mesh(mesh.devices.reshape(8, 4, 4, 2), ("row_0", "row_1", "col_0", "col_1"))
    return jax.shard_map(
        on_device,
        mesh=torus,
        in_specs=(P(ROW_COL, None), P(ROW_COL, None), P()),
        out_specs=(P(), P(ROW_COL, None), P(ROW_COL, None)),
        check_vma=False,
    )
```

profile of v0, /device:TPU:1, one launch (start us, length us, event | category | flops | bytes accessed | tf_op | source)
XLA Modules:
  0.0 286.2 jit_solution(1497360225404504215)
XLA Ops:
  7.2 1.0 fusion.11
  8.2 0.9 fusion.58
  9.1 11.9 %all_gather.18 = bf16[256,512]{1,0:T(8,128)(2,1)} all-gather(bf16[64,512]{1,0:T(8,128)(2,1)S(1)} %fusion.58), channel_id=1, replica_groups=mesh['row_0'=8,'row_1'=4,'col_0'=4,'col_1'=2] {'row_1'}, dimensions={0}, use_global_device_ids=true | all-gather | bytes 327680 | tf_op jit(solution)/shard_map/all_gather | solution.py:29
  21.1 1.0 fusion.12
  22.0 0.9 fusion.59
  23.0 0.8 broadcast_in_dim.39
  23.8 8.4 %all-to-all-start = ((bf16[8,64,512]{2,1,0:T(8,128)(2,1)}), bf16[8,64,512]{2,1,0:T(8,128)(2,1)}, u32[]{:S(2)}, u32[]{:S(2)}) async-start(bf16[8,64,512]{2,1,0:T(8,128)(2,1)} %broadcast_in_dim.39), calls=%async_computation | async-start | bytes 1048576 | tf_op jit(solution)/shard_map/all_to_all | solution.py:20
  32.8 8.9 %all-to-all-done = bf16[8,64,512]{2,1,0:T(8,128)(2,1)} async-done(((bf16[8,64,512]{2,1,0:T(8,128)(2,1)}), bf16[8,64,512]{2,1,0:T(8,128)(2,1)}, u32[]{:S(2)}, u32[]{:S(2)}) %all-to-all-start) | async-done | bytes 524320 | tf_op jit(solution)/shard_map/all_to_all | solution.py:20
  41.8 21.7 %all-gather.6.cloned.1.call-done = bf16[2048,512]{1,0:T(8,128)(2,1)} async-done(((bf16[256,512]{1,0:T(8,128)(2,1)}), bf16[2048,512]{1,0:T(8,128)(2,1)}) %all-gather.6.cloned.1.call-update) | async-done | bytes 2097168 | tf_op jit(solution)/shard_map/all_gather | solution.py:29
  63.5 11.7 %while.30 = (s32[]{:T(128)}, f32[512]{0:T(512)S(1)}, f32[512]{0:T(512)S(1)}, f32[4,512]{1,0:T(4,128)S(1)}, f32[4,512]{1,0:T(4,128)S(1)}, /*index=5*/f32[]{:T(128...) while((s32[]{:T(128)}, f32[512]{0:T(512)S(1)}, ...), condition=%wide.region_7.8_spmd.clone, body=%wide.region_2.7_spmd.clone.sunk | while | flops 270272000 | bytes 3187832 | solution.py:162
  63.5 2.4 fusion.77
  65.9 0.4 exponential_reduce_fusion.3
  66.3 0.1 dynamic_update_slice.18
  66.4 2.4 fusion.77
  68.8 0.4 exponential_reduce_fusion.3
  69.4 2.4 fusion.77
  71.8 0.4 exponential_reduce_fusion.3
  72.3 2.4 fusion.77
  74.7 0.4 exponential_reduce_fusion.3
  75.3 18.5 %all-gather.2 = f32[8,2,2048]{2,1,0:T(2,128)S(1)} all-gather(f32[1,2,2048]{2,1,0:T(2,128)S(1)} %maximum_bitcast_fusion), channel_id=2, replica_groups=mesh['row_0'=8,'row_1'=4,'col_0'=4,'col_1'=2] {'row_0'}, dimensions={0}, use_global_device_ids=true | all-gather | bytes 147456 | tf_op jit(solution)/shard_map/all_gather | solution.py:71
  93.8 0.2 fusion.17
  94.0 9.4 %all-gather.3 = f32[4,2,2048]{2,1,0:T(2,128)S(1)} all-gather(f32[1,2,2048]{2,1,0:T(2,128)S(1)} %maximum_bitcast_fusion.1), channel_id=3, replica_groups=mesh['row_0'=8,'row_1'=4,'col_0'=4,'col_1'=2] {'row_1'}, dimensions={0}, use_global_device_ids=true | all-gather | bytes 81920 | tf_op jit(solution)/shard_map/all_gather | solution.py:71
  103.4 0.2 slice_reduce_fusion.3
  103.7 0.6 broadcast_in_dim.40
  104.3 17.5 %all-to-all-start.1 = ((f32[8,2,512]{2,1,0:T(2,128)}), f32[8,2,512]{2,1,0:T(2,128)S(1)}, u32[]{:S(2)}, u32[]{:S(2)}) async-start(f32[8,2,512]{2,1,0:T(2,128)} %broadcast_in_dim.40), calls=%async_computation.1 | async-start | bytes 65536 | tf_op jit(solution)/shard_map/all_to_all | solution.py:20
  121.9 4.7 %all-to-all-done.1 = f32[8,2,512]{2,1,0:T(2,128)S(1)} async-done(((f32[8,2,512]{2,1,0:T(2,128)}), f32[8,2,512]{2,1,0:T(2,128)S(1)}, u32[]{:S(2)}, u32[]{:S(2)}) %all-to-all-start.1) | async-done | bytes 32800 | tf_op jit(solution)/shard_map/all_to_all | solution.py:20
  126.9 23.7 %while.31 = (s32[]{:T(128)}, f32[512,512]{1,0:T(8,128)}, bf16[4,512,512]{1,2,0:T(8,128)(2,1)S(1)}, f32[]{:T(128)}, bf16[4,512,512]{2,1,0:T(8,128)(2,1)}, /*index...) while((s32[]{:T(128)}, f32[512,512]{1,0:T(8,128)}, ...), condition=%wide.region_16.17_spmd.clone, body=%wide.region_15.16_spmd.clone.sunk | while | flops 539230208 | bytes 5253747 | solution.py:197
  126.9 2.5 bitcast_dynamic-update-slice_fusion.2
  129.4 3.1 %fusion.82 = f32[512,512]{1,0:T(8,128)} fusion(bf16[512,512]{1,0:T(8,128)(2,1)S(1)} %get-tuple-element.337, f32[512,512]{1,0:T(8,128)} %get-tuple-element.380, f32[]{:T(128)} %get-tuple-element.392, pred[]{:T(512)S(6)} %compare.7, bf16[4,512,512]{2,1,0:T(8,128)(2,1)} %get-tuple-element.393, s32[]{:T(128)} %get-tuple-element.379), kind=kOutput, calls=%fused_computation.10.clone.1 | convolution fusion | flops 269221888 | bytes 3146753 | tf_op jit(solution)/shard_map/while/body/eval_jaxpr/dot_general | solution.py:192
  132.6 2.5 bitcast_dynamic-update-slice_fusion.2
  135.1 3.5 %fusion.82 = f32[512,512]{1,0:T(8,128)} fusion(bf16[512,512]{1,0:T(8,128)(2,1)S(1)} %get-tuple-element.337, f32[512,512]{1,0:T(8,128)} %get-tuple-element.380, f32[]{:T(128)} %get-tuple-element.392, pred[]{:T(512)S(6)} %compare.7, bf16[4,512,512]{2,1,0:T(8,128)(2,1)} %get-tuple-element.393, s32[]{:T(128)} %get-tuple-element.379), kind=kOutput, calls=%fused_computation.10.clone.1 | convolution fusion | flops 269221888 | bytes 3146753 | tf_op jit(solution)/shard_map/while/body/eval_jaxpr/dot_general | solution.py:192
  138.6 2.5 bitcast_dynamic-update-slice_fusion.2
  141.1 3.5 %fusion.82 = f32[512,512]{1,0:T(8,128)} fusion(bf16[512,512]{1,0:T(8,128)(2,1)S(1)} %get-tuple-element.337, f32[512,512]{1,0:T(8,128)} %get-tuple-element.380, f32[]{:T(128)} %get-tuple-element.392, pred[]{:T(512)S(6)} %compare.7, bf16[4,512,512]{2,1,0:T(8,128)(2,1)} %get-tuple-element.393, s32[]{:T(128)} %get-tuple-element.379), kind=kOutput, calls=%fused_computation.10.clone.1 | convolution fusion | flops 269221888 | bytes 3146753 | tf_op jit(solution)/shard_map/while/body/eval_jaxpr/dot_general | solution.py:192
  144.6 2.5 bitcast_dynamic-update-slice_fusion.2
  147.1 3.5 %fusion.82 = f32[512,512]{1,0:T(8,128)} fusion(bf16[512,512]{1,0:T(8,128)(2,1)S(1)} %get-tuple-element.337, f32[512,512]{1,0:T(8,128)} %get-tuple-element.380, f32[]{:T(128)} %get-tuple-element.392, pred[]{:T(512)S(6)} %compare.7, bf16[4,512,512]{2,1,0:T(8,128)(2,1)} %get-tuple-element.393, s32[]{:T(128)} %get-tuple-element.379), kind=kOutput, calls=%fused_computation.10.clone.1 | convolution fusion | flops 269221888 | bytes 3146753 | tf_op jit(solution)/shard_map/while/body/eval_jaxpr/dot_general | solution.py:192
  150.6 4.2 %convolution_multiply_fusion.3 = f32[2048,512]{1,0:T(8,128)} fusion(bf16[2048,512]{1,0:T(8,128)(2,1)S(1)} %bitcast.243, bf16[512,512]{1,0:T(8,128)(2,1)} %bitcast.2, f32[]{:T(128)} %bitcast.241), kind=kOutput, calls=%fused_computation.21 | convolution fusion | flops 1074790400 | bytes 6815748 | tf_op jit(solution)/shard_map/dot_general | solution.py:200
  154.9 51.6 %reduce-scatter.3.cloned.1.call-done = f32[256,512]{1,0:T(8,128)} async-done(((f32[2048,512]{1,0:T(8,128)}), f32[256,512]{1,0:T(8,128)}) %reduce-scatter.3.cloned.1.call-update) | async-done | bytes 524304 | tf_op jit(solution)/shard_map/reduce_scatter | solution.py:97
  206.5 4.9 %all-to-all-start.2 = ((f32[8,64,512]{2,1,0:T(8,128)}), f32[8,64,512]{2,1,0:T(8,128)S(1)}, u32[]{:S(2)}, u32[]{:S(2)}) async-start(f32[8,64,512]{2,1,0:T(8,128)} %bitcast.35), calls=%async_computation.2 | async-start | bytes 2097152 | tf_op jit(solution)/shard_map/all_to_all | solution.py:109
  211.4 15.1 %all-to-all-done.2 = f32[8,64,512]{2,1,0:T(8,128)S(1)} async-done(((f32[8,64,512]{2,1,0:T(8,128)}), f32[8,64,512]{2,1,0:T(8,128)S(1)}, u32[]{:S(2)}, u32[]{:S(2)}) %all-to-all-start.2) | async-done | bytes 1048608 | tf_op jit(solution)/shard_map/all_to_all | solution.py:109
  226.5 0.1 reduce_sum.95
  226.6 3.4 %reduce-scatter.5.cloned.1.call-done = f32[64,512]{1,0:T(8,128)} async-done(((f32[256,512]{1,0:T(8,128)}), f32[64,512]{1,0:T(8,128)}) %reduce-scatter.5.cloned.1.call-update) | async-done | bytes 131088 | tf_op jit(solution)/shard_map/reduce_scatter | solution.py:97
  230.0 1.2 multiply_reduce_fusion
  231.2 0.7 subtract_reduce_fusion
  233.2 14.2 %psum.28 = f32[]{:T(128)} all-reduce(f32[]{:T(128)S(6)} %add.191), channel_id=1, replica_groups=mesh['row_0'=8,'row_1'=4,'col_0'=4,'col_1'=2] {'row_0'}, use_global_device_ids=true, to_apply=%region_11.12 | all-reduce | flops 1 | bytes 8 | tf_op jit(solution)/shard_map/psum | solution.py:91
  247.4 7.5 %psum.29 = f32[]{:T(128)} all-reduce(f32[]{:T(128)} %psum.28), channel_id=1, replica_groups=mesh['row_0'=8,'row_1'=4,'col_0'=4,'col_1'=2] {'row_1'}, use_global_device_ids=true, to_apply=%region_12.13 | all-reduce | flops 1 | bytes 8 | tf_op jit(solution)/shard_map/psum | solution.py:91
  254.9 9.0 %psum.30 = f32[]{:T(128)} all-reduce(f32[]{:T(128)} %psum.29), channel_id=1, replica_groups=mesh['row_0'=8,'row_1'=4,'col_0'=4,'col_1'=2] {'col_0'}, use_global_device_ids=true, to_apply=%region_13.14 | all-reduce | flops 1 | bytes 8 | tf_op jit(solution)/shard_map/psum | solution.py:91
  263.8 12.3 %psum.31 = f32[]{:T(128)} all-reduce(f32[]{:T(128)} %psum.30), channel_id=1, replica_groups=mesh['row_0'=8,'row_1'=4,'col_0'=4,'col_1'=2] {'col_1'}, use_global_device_ids=true, to_apply=%region_14.15 | all-reduce | flops 1 | bytes 8 | tf_op jit(solution)/shard_map/psum | solution.py:91
  276.8 1.7 subtract_divide_fusion
  (71 shorter events, 1.1 us)
Async XLA Ops:
  7.2 56.3 %all-gather.6.cloned.1.call-start = ((), (), s32[]{:S(2)}) async-start(), calls=%async_computation.5 | async-start | bytes 2359296 | tf_op jit(solution)/shard_map/all_gather | solution.py:29
  23.8 18.0 %all-to-all-start = ((bf16[8,64,512]{2,1,0:T(8,128)(2,1)}), bf16[8,64,512]{2,1,0:T(8,128)(2,1)}, u32[]{:S(2)}, u32[]{:S(2)}) async-start(bf16[8,64,512]{2,1,0:T(8,128)(2,1)} %broadcast_in_dim.39), calls=%async_computation | async-start | bytes 1048576 | tf_op jit(solution)/shard_map/all_to_all | solution.py:20
  104.3 22.2 %all-to-all-start.1 = ((f32[8,2,512]{2,1,0:T(2,128)}), f32[8,2,512]{2,1,0:T(2,128)S(1)}, u32[]{:S(2)}, u32[]{:S(2)}) async-start(f32[8,2,512]{2,1,0:T(2,128)} %broadcast_in_dim.40), calls=%async_computation.1 | async-start | bytes 65536 | tf_op jit(solution)/shard_map/all_to_all | solution.py:20
  121.8 84.7 %reduce-scatter.3.cloned.1.call-start = ((), (), s32[]{:S(2)}) async-start(), calls=%async_computation.6 | async-start | bytes 4718592 | tf_op jit(solution)/shard_map/reduce_scatter | solution.py:97
  154.8 75.1 %copy-start = (bf16[64,512]{1,0:T(8,128)(2,1)S(1)}, bf16[64,512]{1,0:T(8,128)(2,1)}, u32[]{:S(2)}) copy-start(bf16[64,512]{1,0:T(8,128)(2,1)} %param.8) | copy-start | bytes 196612
  154.8 75.1 %copy-start.1 = (bf16[64,512]{1,0:T(8,128)(2,1)S(1)}, bf16[64,512]{1,0:T(8,128)(2,1)}, u32[]{:S(2)}) copy-start(bf16[64,512]{1,0:T(8,128)(2,1)} %param.7) | copy-start | bytes 196612
  154.9 75.1 %reduce-scatter.5.cloned.1.call-start = ((), (), s32[]{:S(2)}) async-start(), calls=%async_computation.7 | async-start | bytes 655360 | tf_op jit(solution)/shard_map/reduce_scatter | solution.py:97
  206.5 20.0 %all-to-all-start.2 = ((f32[8,64,512]{2,1,0:T(8,128)}), f32[8,64,512]{2,1,0:T(8,128)S(1)}, u32[]{:S(2)}, u32[]{:S(2)}) async-start(f32[8,64,512]{2,1,0:T(8,128)} %bitcast.35), calls=%async_computation.2 | async-start | bytes 2097152 | tf_op jit(solution)/shard_map/all_to_all | solution.py:109
Sparse Core Ops, SparseCore 0:
  21.2 42.2 all-gather.5
  155.0 51.5 reduce-scatter.2
  209.1 20.8 reduce-scatter.4
where the time goes:
time: 287 us; the launch traced here: 286 us
  waiting for transfers between devices  105 us (37%)
  blocking collectives  82.8 us (29%)
  matrix products  37.4 us (13%)
  starting transfers between devices  30.8 us (11%)
  between operations  17.6 us (6%)
  other arithmetic  9.43 us (3%)
    reduce_scatter x2, waiting for transfers between devices, sum_by_axis(): total = lax.psum_scatter(total, axis, scatter_dimension=0, tiled=True)  55 us
    psum x4, blocking collectives, over_axes(): value = lax.psum(value, axis)  43 us
    all_gather x2, blocking collectives, all_in_one_2(): both, at, found = (lax.all_gather(jnp.concatenate(lines), axis), 0, {})  27.9 us
    all_to_all x2, starting transfers between devices, from_everyone(): return lax.all_to_all(copies, axis, split_axis=0, concat_axis=0, tiled=True)  25.9 us
    all_gather x1, waiting for transfers between devices, gather_axes(): value = lax.all_gather(value, axis, axis=dim, tiled=True)  21.7 us
    dot_general x8, matrix products, scores(): jnp.einsum('re,ce->rc', img_tile, txt_block, preferred_element_type=jnp.f...  19.6 us
    all_to_all x1, waiting for transfers between devices, summed_on_arrival(): tiles = lax.all_to_all(in_blocks(value, dim, count), axis, 0, 0, tiled=True)  15.1 us
    all_to_all x2, waiting for transfers between devices, from_everyone(): return lax.all_to_all(copies, axis, split_axis=0, concat_axis=0, tiled=True)  13.6 us
  transfers between devices with their start and end apart: 6, of which 6 were waited for; matrix products, arithmetic and copies ran while one was open for 1% of the time, Pallas kernels for 0%

commit v1 on v0

v1 whole, which is shorter than its diff:
```python
import functools
import math

import jax
import jax.numpy as jnp
from jax import lax
from jax.experimental import pallas as pl
from jax.experimental.pallas import tpu as pltpu
from jax.sharding import Mesh
from jax.sharding import PartitionSpec as P

MESH = pl.DeviceIdType.MESH
AXES = ("z", "y", "x", "core")
SIZE = {"z": 8, "y": 4, "x": 4, "core": 2}
NT = (((1,), (1,)), ((), ()))
TN = (((0,), (0,)), ((), ()))
NN = (((1,), (0,)), ((), ()))

LINE = [(k, d) for k in range(2) for d in range(8)]
PLANE = [(dy, dx) for dy in range(4) for dx in range(4)]


def at_line(k, d):
    return {
        "z": lax.rem(lax.axis_index("z") + d, 8),
        "core": lax.rem(lax.axis_index("core") + k, 2),
    }


def at_plane(dy, dx):
    return {
        "y": lax.rem(lax.axis_index("y") + dy, 4),
        "x": lax.rem(lax.axis_index("x") + dx, 4),
    }


def back_line(k, d):
    return k * 8 + (8 - d) % 8


def back_plane(dy, dx):
    return ((4 - dy) % 4) * 4 + (4 - dx) % 4


def kernel(
    batch, image_ref, text_ref, scale_ref, loss_ref, img_grad_ref, txt_grad_ref,
    img, txt, half, weights, row_part, row_scale, col_hi, col_lo,
    row_stat, col_stat, row_loss, col_loss,
    img_out, img_pair, txt_out, img_in, txt_in, img_own, txt_own,
    img_s, img_r, pair_s, pair_r, txt_s, txt_r,
    rstat_s, rstat_r, cstat_s, cstat_r, rloss_s, rloss_r, closs_s, closs_r,
    pg_s, pg_r, ig_s, ig_r, tg_s, tg_r,
):
    n = 64
    scale = scale_ref[0]

    def copy(src, dst, s, r, to):
        return pltpu.make_async_remote_copy(
            src_ref=src, dst_ref=dst, send_sem=s, recv_sem=r, device_id=to, device_id_type=MESH
        )

    barrier = pltpu.get_barrier_semaphore()
    for k, d in LINE[1:]:
        pl.semaphore_signal(barrier, inc=1, device_id=at_line(k, d), device_id_type=MESH)
    for dy, dx in PLANE[1:]:
        pl.semaphore_signal(barrier, inc=1, device_id=at_plane(dy, dx), device_id_type=MESH)

    def normal(ref):
        wide = ref[...].astype(jnp.float32)
        length = jnp.sqrt(jnp.sum(wide * wide, axis=1, keepdims=True) + 1e-6)
        return wide / length, length

    unit_image, image_len = normal(image_ref)
    unit_text, text_len = normal(text_ref)
    img[0] = unit_image.astype(jnp.bfloat16)
    txt[0] = unit_text.astype(jnp.bfloat16)
    pl.semaphore_wait(barrier, 30)

    sends = []
    for dy, dx in PLANE[1:]:
        b = back_plane(dy, dx)
        c = copy(txt.at[0], txt.at[b], txt_s.at[b], txt_r.at[b], at_plane(dy, dx))
        c.start()
        sends.append(c)
    for d in (4, 3, 5, 2, 6, 1, 7):
        b = back_line(0, d)
        c = copy(img.at[0], img.at[b], img_s.at[b], img_r.at[b], at_line(0, d))
        c.start()
        sends.append(c)
    pairs = []
    for d in (0, 1, 7, 2, 6, 3, 5, 4):
        if d:
            copy(img.at[d], img.at[d], img_s.at[d], img_r.at[d], at_line(0, 0)).wait_recv()
        c = copy(img.at[d], img.at[8 + d], pair_s.at[d], pair_r.at[d], at_line(1, 0))
        c.start()
        pairs.append(c)
    for d in range(8):
        pairs[d].wait_recv()
    for j in range(1, 16):
        copy(txt.at[j], txt.at[j], txt_s.at[j], txt_r.at[j], at_plane(0, 0)).wait_recv()

    power = scale * (0.5 * math.log2(math.e))
    down, up = math.exp(-15.0), math.exp(15.0)
    col_hi[...] = jnp.zeros_like(col_hi)
    col_lo[...] = jnp.zeros_like(col_lo)

    def strip(i, carry):
        r = pl.multiple_of(i * 128, 128)
        rows = img[pl.ds(2 * i, 2)].reshape(128, 512)
        hi_row = jnp.zeros((128, 128), jnp.float32)
        lo_row = jnp.zeros((128, 128), jnp.float32)
        for q in range(4):
            cols = txt[q * 4 : q * 4 + 4].reshape(256, 512)
            dots = lax.dot_general(rows, cols, NT, preferred_element_type=jnp.float32)
            f = jnp.exp2(dots * power)
            half[pl.ds(r, 128), q * 256 : q * 256 + 256] = f
            hi = f * down
            hi = hi * hi
            lo = jnp.minimum(f, 1.0) * up
            lo = lo * lo
            hi_row = hi_row + (hi[:, :128] + hi[:, 128:])
            lo_row = lo_row + (lo[:, :128] + lo[:, 128:])
            col_hi[:, q * 256 : q * 256 + 256] += jnp.sum(hi.reshape(16, 8, 256), axis=0)
            col_lo[:, q * 256 : q * 256 + 256] += jnp.sum(lo.reshape(16, 8, 256), axis=0)
        row_part[0, pl.ds(r, 128), :] = hi_row
        row_part[1, pl.ds(r, 128), :] = lo_row
        return carry

    lax.fori_loop(0, 8, strip, 0)

    def log_of(hi, lo):
        return jnp.where(
            hi >= math.exp(-30.0), jnp.log(hi) + 30.0, jnp.log(lo) - 30.0
        )

    row_hi = jnp.sum(row_part[0].T, axis=0, keepdims=True)
    row_lo = jnp.sum(row_part[1].T, axis=0, keepdims=True)
    row_stat[0, :, :1024] = log_of(row_hi, row_lo)
    same = img[0].astype(jnp.float32) * txt[0].astype(jnp.float32)
    positive = scale * jnp.sum(same)
    row_stat[0, :, 1024:] = jnp.full((1, 128), positive, jnp.float32)
    for k, d in LINE[1:]:
        b = back_line(k, d)
        c = copy(row_stat.at[0], row_stat.at[b], rstat_s.at[b], rstat_r.at[b], at_line(k, d))
        c.start()
        sends.append(c)
    col_stat[0] = log_of(
        jnp.sum(col_hi[...], axis=0, keepdims=True), jnp.sum(col_lo[...], axis=0, keepdims=True)
    )
    for dy, dx in PLANE[1:]:
        b = back_plane(dy, dx)
        c = copy(col_stat.at[0], col_stat.at[b], cstat_s.at[b], cstat_r.at[b], at_plane(dy, dx))
        c.start()
        sends.append(c)
    for j in range(1, 16):
        copy(row_stat.at[j], row_stat.at[j], rstat_s.at[j], rstat_r.at[j], at_line(0, 0)).wait_recv()
    for j in range(1, 16):
        copy(col_stat.at[j], col_stat.at[j], cstat_s.at[j], cstat_r.at[j], at_plane(0, 0)).wait_recv()

    def row_order(j):
        k, d = j // 8, j % 8
        parts = row_stat[j, :, :1024]
        pieces = [None] * 16
        for k2, d2 in LINE:
            here = ((k + k2) % 2) * 8 + (d + d2) % 8
            there = k2 * 8 + d2
            pieces[here] = parts[:, there * n : there * n + n]
        return jnp.concatenate(pieces, axis=1)

    def col_order(j):
        y0, x0 = j // 4, j % 4
        parts = col_stat[j]
        pieces = [None] * 16
        for y2, x2 in PLANE:
            here = ((y0 + y2) % 4) * 4 + (x0 + x2) % 4
            there = y2 * 4 + x2
            pieces[here] = parts[:, there * n : there * n + n]
        return jnp.concatenate(pieces, axis=1)

    def merged(parts):
        summit = functools.reduce(jnp.maximum, parts)
        total = sum(jnp.exp(p - summit) for p in parts)
        return summit + jnp.log(total)

    row_lse = merged([row_order(j) for j in range(16)])
    col_lse = merged([col_order(j) for j in range(16)])
    all_positive = sum(row_stat[j, :, 1024:] for j in range(16))
    row_loss[0] = jnp.full((1, 128), jnp.sum(row_lse), jnp.float32) - 2.0 * all_positive
    col_loss[0] = jnp.full((1, 128), jnp.sum(col_lse), jnp.float32)
    for dy, dx in PLANE[1:]:
        b = back_plane(dy, dx)
        c = copy(row_loss.at[0], row_loss.at[b], rloss_s.at[b], rloss_r.at[b], at_plane(dy, dx))
        c.start()
        sends.append(c)
    for k, d in LINE[1:]:
        b = back_line(k, d)
        c = copy(col_loss.at[0], col_loss.at[b], closs_s.at[b], closs_r.at[b], at_line(k, d))
        c.start()
        sends.append(c)

    root = math.sqrt(0.5)
    row_factor = jnp.exp(row_lse * -0.5) * root
    col_factor = jnp.exp(col_lse * -0.5) * root
    row_scale[...] = jnp.broadcast_to(row_factor, (128, 1024)).T

    def weigh(i, carry):
        r = pl.multiple_of(i * 64, 64)
        a = row_scale[pl.ds(r, 64), :]
        for q in range(8):
            f = half[pl.ds(r, 64), q * 128 : q * 128 + 128]
            by_row = f * a
            by_col = f * col_factor[:, q * 128 : q * 128 + 128]
            weights[pl.ds(r, 64), q * 128 : q * 128 + 128] = (
                by_row * by_row + by_col * by_col
            ).astype(jnp.bfloat16)
        return carry

    lax.fori_loop(0, 16, weigh, 0)

    texts = txt[...].reshape(1024, 512)
    images = img[...].reshape(1024, 512)
    pair_sends = []
    for h in range(2):
        part = jnp.dot(
            weights[512 + h * 256 : 768 + h * 256, :], texts, preferred_element_type=jnp.float32
        )
        img_out[1, 4 * h : 4 * h + 4] = part.astype(jnp.bfloat16).reshape(4, 64, 512)
        c = copy(
            img_out.at[1, pl.ds(4 * h, 4)], img_pair.at[pl.ds(4 * h, 4)],
            pg_s.at[h], pg_r.at[h], at_line(1, 0),
        )
        c.start()
        pair_sends.append(c)
    for h in range(4):
        part = lax.dot_general(
            weights[:, h * 256 : h * 256 + 256], images, TN, preferred_element_type=jnp.float32
        )
        if h == 0:
            txt_own[...] = part[:64]
        txt_out[4 * h : 4 * h + 4] = part.astype(jnp.bfloat16).reshape(4, 64, 512)
        for j in range(4 * h, 4 * h + 4):
            if j:
                dy, dx = PLANE[j]
                b = back_plane(dy, dx)
                c = copy(txt_out.at[j], txt_in.at[b], tg_s.at[b], tg_r.at[b], at_plane(dy, dx))
                c.start()
                sends.append(c)
    for h in (1, 0):
        part = jnp.dot(weights[h * 256 : h * 256 + 256, :], texts, preferred_element_type=jnp.float32)
        pair_sends[h].wait_recv()
        part = part + img_pair[4 * h : 4 * h + 4].astype(jnp.float32).reshape(256, 512)
        if h == 0:
            img_own[...] = part[:64]
        img_out[0, 4 * h : 4 * h + 4] = part.astype(jnp.bfloat16).reshape(4, 64, 512)
        for d in range(4 * h, 4 * h + 4):
            if d:
                b = back_line(0, d)
                c = copy(img_out.at[0, d], img_in.at[b], ig_s.at[b], ig_r.at[b], at_line(0, d))
                c.start()
                sends.append(c)

    def finish(own, parts, other, unit, length):
        total = own[...]
        for part in parts:
            total = total + part.astype(jnp.float32)
        gradient = scale * total - scale * other.astype(jnp.float32)
        return (gradient - unit * jnp.sum(unit * gradient, axis=1, keepdims=True)) / length

    for d in range(1, 8):
        copy(img_in.at[d], img_in.at[d], ig_s.at[d], ig_r.at[d], at_line(0, 0)).wait_recv()
    img_grad_ref[...] = finish(
        img_own, [img_in[d] for d in range(1, 8)], txt[0], unit_image, image_len
    )
    for j in range(1, 16):
        copy(txt_in.at[j], txt_in.at[j], tg_s.at[j], tg_r.at[j], at_plane(0, 0)).wait_recv()
    txt_grad_ref[...] = finish(
        txt_own, [txt_in[j] for j in range(1, 16)], img[0], unit_text, text_len
    )
    for j in range(1, 16):
        copy(row_loss.at[j], row_loss.at[j], rloss_s.at[j], rloss_r.at[j], at_line(0, 0)).wait_recv()
        copy(col_loss.at[j], col_loss.at[j], closs_s.at[j], closs_r.at[j], at_line(0, 0)).wait_recv()
    total = sum(row_loss[j] + col_loss[j] for j in range(16))
    loss_ref[...] = total / (2.0 * batch)
    for c in sends + pairs + pair_sends:
        c.wait_send()


def on_device(image, text, logit_scale):
    batch = image.shape[0] * 256
    f32, bf16 = jnp.float32, jnp.bfloat16
    dma = pltpu.SemaphoreType.DMA
    vmem = pltpu.VMEM
    loss, img_grad, txt_grad = pl.pallas_call(
        functools.partial(kernel, batch),
        out_shape=(
            jax.ShapeDtypeStruct((1, 128), f32),
            jax.ShapeDtypeStruct((64, 512), f32),
            jax.ShapeDtypeStruct((64, 512), f32),
        ),
        in_specs=[
            pl.BlockSpec(memory_space=vmem),
            pl.BlockSpec(memory_space=vmem),
            pl.BlockSpec(memory_space=pltpu.SMEM),
        ],
        out_specs=[pl.BlockSpec(memory_space=vmem)] * 3,
        scratch_shapes=[
            vmem((16, 64, 512), bf16),
            vmem((16, 64, 512), bf16),
            vmem((1024, 1024), f32),
            vmem((1024, 1024), bf16),
            vmem((2, 1024, 128), f32),
            vmem((1024, 128), f32),
            vmem((8, 1024), f32),
            vmem((8, 1024), f32),
            vmem((16, 1, 1152), f32),
            vmem((16, 1, 1024), f32),
            vmem((16, 1, 128), f32),
            vmem((16, 1, 128), f32),
            vmem((2, 8, 64, 512), bf16),
            vmem((8, 64, 512), bf16),
            vmem((16, 64, 512), bf16),
            vmem((8, 64, 512), bf16),
            vmem((16, 64, 512), bf16),
            vmem((64, 512), f32),
            vmem((64, 512), f32),
            dma((8,)), dma((8,)), dma((8,)), dma((8,)), dma((16,)), dma((16,)),
            dma((16,)), dma((16,)), dma((16,)), dma((16,)), dma((16,)), dma((16,)), dma((16,)), dma((16,)),
            dma((2,)), dma((2,)), dma((8,)), dma((8,)), dma((16,)), dma((16,)),
        ],
        compiler_params=pltpu.CompilerParams(
            collective_id=0, has_side_effects=True, vmem_limit_bytes=56 * 2**20
        ),
        cost_estimate=pl.CostEstimate(
            flops=6 * 1024 * 1024 * 512, bytes_accessed=400000, transcendentals=1024 * 1024
        ),
        name="contrast",
    )(image, text, logit_scale)
    return loss[0, :1], img_grad, txt_grad


def solution(mesh):
    torus = Mesh(mesh.devices.reshape(8, 4, 4, 2), AXES)
    return jax.shard_map(
        on_device,
        mesh=torus,
        in_specs=(P(AXES, None), P(AXES, None), P()),
        out_specs=(P(), P(AXES, None), P(AXES, None)),
        check_vma=False,
    )
```

time: 287 us -> 64.6 us (0.23)
  waiting for transfers between devices: 105 us -> 0 us
  blocking collectives: 82.8 us -> 0 us
  Pallas kernels: 0 us -> 59.1 us
  matrix products: 37.4 us -> 0 us
  starting transfers between devices: 30.8 us -> 0 us
  between operations: 17.6 us -> 2.47 us
  other arithmetic: 9.43 us -> 0 us
    pallas_call x0 -> x1, Pallas kernels: none -> 59.1 us  [on_device(): pl.pallas_call(functools.partial(kernel, batch), out_shape=(jax.ShapeDtyp...]
    reduce_scatter x2 -> x0, waiting for transfers between devices: 55 us -> none  [sum_by_axis(): total = lax.psum_scatter(total, axis, scatter_dimension=0, tiled=True)]
    psum x4 -> x0, blocking collectives: 43 us -> none  [over_axes(): value = lax.psum(value, axis)]
    all_gather x3 -> x0, blocking collectives: 39.8 us -> none  [the longest x2 27.9 us: all_in_one_2(): both, at, found = (lax.all_gather(jnp.concatenate(lines), axis), 0, {})]
    dot_general x13 -> x0, matrix products: 37.4 us -> none  [the longest x8 19.6 us: scores(): jnp.einsum('re,ce->rc', img_tile, txt_block, preferred_element_type=jnp.f...]
    all_to_all x3 -> x0, starting transfers between devices: 30.7 us -> none  [the longest x2 25.9 us: from_everyone(): return lax.all_to_all(copies, axis, split_axis=0, concat_axis=0, tiled=True)]
    all_to_all x3 -> x0, waiting for transfers between devices: 28.7 us -> none  [the longest x1 15.1 us: summed_on_arrival(): tiles = lax.all_to_all(in_blocks(value, dim, count), axis, 0, 0, tiled=True)]
    all_gather x1 -> x0, waiting for transfers between devices: 21.7 us -> none  [gather_axes(): value = lax.all_gather(value, axis, axis=dim, tiled=True)]
  transfers between devices with their start and end apart: 6 -> 0, of which waited for: 6 -> 0; matrix products, arithmetic and copies ran while one was open for 1% -> 0% of each run, Pallas kernels for 0% -> 0%
where the time goes in v1:
time: 64.6 us; the launch traced here: 64.5 us
  Pallas kernels  59.1 us (91%)
  local copies, waits for them, and re-layouts  2.93 us (5%)
  between operations  2.47 us (4%)
    pallas_call x1, Pallas kernels, on_device(): pl.pallas_call(functools.partial(kernel, batch), out_shape=(jax.ShapeDtyp...  59.1 us
    unnamed x6, local copies, waits for them, and re-layouts  2.93 us

profile of v1, /device:TPU:1, one launch (start us, length us, event | category | flops | bytes accessed | tf_op | source)
XLA Modules:
  0.0 64.5 jit_solution(12720836859680393845)
XLA Ops:
  1.3 59.1 %contrast.1 = (f32[1,128]{1,0:T(1,128)}, f32[64,512]{1,0:T(8,128)}, f32[64,512]{1,0:T(8,128)}) custom-call(bf16[64,512]{1,0:T(8,128)(2,1)} %image_ref.1, bf16[64,512]{1,0:T(8,128)(2,1)} %text_ref.1, f32[1]{0:T(128)S(6)} %copy.9.scale_ref), custom_call_target="tpu_custom_call" | custom-call | flops 3221225472 | bytes 400000 | tf_op jit(solution)/shard_map/contrast/pallas_call | solution.py:293
  60.3 0.0 copy-start.1
  60.4 0.7 %copy-done.1 = f32[1,128]{1,0:T(1,128)S(1)} copy-done((f32[1,128]{1,0:T(1,128)S(1)}, f32[1,128]{1,0:T(1,128)}, u32[]{:S(2)}) %copy-start.1) | copy-done | bytes 536
  61.1 0.0 copy-start
  61.1 1.6 %copy.11 = f32[64,512]{1,0:T(8,128)} copy(f32[64,512]{1,0:T(8,128)} %get-tuple-element.13) | data formatting | bytes 262144
  62.7 0.0 copy-done
  62.7 0.7 %copy.12 = f32[64,512]{1,0:T(8,128)} copy(f32[64,512]{1,0:T(8,128)S(1)} %copy-done) | data formatting | bytes 262144
Async XLA Ops:
  60.3 0.7 %copy-start.1 = (f32[1,128]{1,0:T(1,128)S(1)}, f32[1,128]{1,0:T(1,128)}, u32[]{:S(2)}) copy-start(f32[1,128]{1,0:T(1,128)} %get-tuple-element.6) | copy-start | bytes 1540
  61.1 1.6 %copy-start = (f32[64,512]{1,0:T(8,128)S(1)}, f32[64,512]{1,0:T(8,128)}, u32[]{:S(2)}) copy-start(f32[64,512]{1,0:T(8,128)} %get-tuple-element.14) | copy-start | bytes 393220

commit v2 on v1

v2 whole, which is shorter than its diff:
```python
import functools
import math

import jax
import jax.numpy as jnp
from jax import lax
from jax.experimental import pallas as pl
from jax.experimental.pallas import tpu as pltpu
from jax.sharding import Mesh
from jax.sharding import PartitionSpec as P

MESH = pl.DeviceIdType.MESH
AXES = ("z", "y", "x", "core")
SIZE = {"z": 8, "y": 4, "x": 4, "core": 2}
NT = (((1,), (1,)), ((), ()))
TN = (((0,), (0,)), ((), ()))
NN = (((1,), (0,)), ((), ()))

NEAR = [0, 2, 6, 1, 7]
FAR = [3, 5, 4]
LINE = [(0, d) for d in NEAR] + [(1, d) for d in NEAR] + [(0, d) for d in FAR] + [(1, d) for d in FAR]
PLANE = [
    (0, 0), (0, 1), (0, 3), (1, 0), (3, 0), (0, 2), (2, 0), (1, 1),
    (1, 3), (3, 1), (3, 3), (1, 2), (3, 2), (2, 1), (2, 3), (2, 2),
]
ISLOT = {p: j for j, p in enumerate(LINE)}
TSLOT = {p: j for j, p in enumerate(PLANE)}
ROUND = (2, 1, 3)


def at_line(k, d):
    return {
        "z": lax.rem(lax.axis_index("z") + d, 8),
        "core": lax.rem(lax.axis_index("core") + k, 2),
    }


def at_plane(dy, dx):
    return {
        "y": lax.rem(lax.axis_index("y") + dy, 4),
        "x": lax.rem(lax.axis_index("x") + dx, 4),
    }


def kernel(
    batch, image_ref, text_ref, scale_ref, loss_ref, img_grad_ref, txt_grad_ref,
    raw_img, raw_txt, raw_scale, img, txt, half, weights, row_part, row_scale, col_hi, col_lo,
    row_stat, col_stat, row_loss, col_loss,
    img_out, img_pair, img_hold, img_mid, img_send, img_in, img_own,
    txt_out, txt_mid, txt_send, txt_in,
    load, txt_s, txt_r, img_s, img_r, pair_s, pair_r,
    rstat_s, rstat_r, cstat_s, cstat_r, rloss_s, rloss_r, closs_s, closs_r,
    pg_s, pg_r, im_s, im_r, ig_s, ig_r, tm_s, tm_r, tg_s, tg_r,
):
    n = 64
    f32, bf16 = jnp.float32, jnp.bfloat16

    def copy(src, dst, s, r, to):
        return pltpu.make_async_remote_copy(
            src_ref=src, dst_ref=dst, send_sem=s, recv_sem=r, device_id=to, device_id_type=MESH
        )

    barrier = pltpu.get_barrier_semaphore()
    for k, d in LINE[1:]:
        pl.semaphore_signal(barrier, inc=1, device_id=at_line(k, d), device_id_type=MESH)
    for dy, dx in PLANE[1:]:
        pl.semaphore_signal(barrier, inc=1, device_id=at_plane(dy, dx), device_id_type=MESH)
    loads = [
        pltpu.make_async_copy(image_ref, raw_img, load.at[0]),
        pltpu.make_async_copy(text_ref, raw_txt, load.at[1]),
        pltpu.make_async_copy(scale_ref, raw_scale, load.at[2]),
    ]
    for c in loads:
        c.start()
    col_hi[...] = jnp.zeros_like(col_hi)
    col_lo[...] = jnp.zeros_like(col_lo)
    row_part[...] = jnp.zeros_like(row_part)
    for c in loads:
        c.wait()
    scale = raw_scale[0]

    def normal(ref):
        wide = ref[...].astype(f32)
        length = jnp.sqrt(jnp.sum(wide * wide, axis=1, keepdims=True) + 1e-6)
        return wide / length, length

    img[0] = normal(raw_img)[0].astype(bf16)
    txt[0] = normal(raw_txt)[0].astype(bf16)
    pl.semaphore_wait(barrier, 30)

    sends = []

    def rows(h):
        return pl.ds(32 * h, 32)

    def go(c):
        c.start()
        sends.append(c)

    def text_part(slot, h):
        j = TSLOT[slot]
        return txt.at[j, rows(h)], txt_s.at[2 * j + h], txt_r.at[2 * j + h]

    def send_text(source, h, dy, dx):
        landing = ((source[0] - dy) % 4, (source[1] - dx) % 4)
        dst, s, r = text_part(landing, h)
        go(copy(text_part(source, h)[0], dst, s, r, at_plane(dy, dx)))

    def image_part(d, h):
        return img.at[ISLOT[0, d], rows(h)], img_s.at[2 * d + h], img_r.at[2 * d + h]

    def send_image(source, h, d):
        dst, s, r = image_part((source - d) % 8, h)
        go(copy(image_part(source, h)[0], dst, s, r, at_line(0, d)))

    arrived = set()

    def need_text(slot, h):
        if slot != (0, 0) and (slot, h) not in arrived:
            arrived.add((slot, h))
            part, s, r = text_part(slot, h)
            copy(part, part, s, r, at_plane(0, 1)).wait_recv()

    def need_image(d, h):
        if d and (d, h) not in arrived:
            arrived.add((d, h))
            part, s, r = image_part(d, h)
            copy(part, part, s, r, at_line(0, 1)).wait_recv()

    pairs = {}

    def send_pair(d):
        need_image(d, 0)
        need_image(d, 1)
        pairs[d] = copy(
            img.at[ISLOT[0, d]], img.at[ISLOT[1, d]], pair_s.at[d], pair_r.at[d], at_line(1, 0)
        )
        go(pairs[d])

    def spread(source, h):
        need_text(source, h)
        for d in ROUND:
            send_text(source, h, *((d, 0) if h == 0 else (0, d)))

    def relay(source, h):
        need_image(source, h)
        if source == 6:
            if h == 0:
                send_image(6, 0, 2)
            send_image(6, h, 1)
        else:
            if h == 1:
                send_image(2, 1, 6)
            send_image(2, h, 7)

    send_image(0, 0, 2)
    send_image(0, 0, 6)
    for d in ROUND:
        send_text((0, 0), 0, 0, d)
        send_text((0, 0), 1, d, 0)
    send_image(0, 1, 2)
    send_image(0, 1, 6)
    spread((0, 0), 0)
    spread((0, 0), 1)
    for h in range(2):
        send_image(0, h, 1)
        send_image(0, h, 7)
    send_pair(0)
    for d in (3, 1):
        spread((0, d), 0)
        spread((d, 0), 1)
    relay(6, 0)
    relay(2, 0)
    spread((0, 2), 0)
    spread((2, 0), 1)
    relay(6, 1)
    relay(2, 1)
    for d in (2, 6, 1, 7):
        send_pair(d)

    power = scale * (0.5 * math.log2(math.e))
    down, up = math.exp(-15.0), math.exp(15.0)

    def strip(i, g):
        r = pl.multiple_of(i * 128, 128)
        c = pl.multiple_of(g * 256, 256)
        left = img[pl.ds(2 * i, 2)].reshape(128, 512)
        right = txt[pl.ds(4 * g, 4)].reshape(256, 512)
        dots = lax.dot_general(left, right, NT, preferred_element_type=f32)
        f = jnp.exp2(dots * power)
        half[pl.ds(r, 128), pl.ds(c, 256)] = f
        hi = f * down
        hi = hi * hi
        lo = jnp.minimum(f, 1.0) * up
        lo = lo * lo
        row_part[0, pl.ds(r, 128), :] += hi[:, :128] + hi[:, 128:]
        row_part[1, pl.ds(r, 128), :] += lo[:, :128] + lo[:, 128:]
        col_hi[:, pl.ds(c, 256)] += jnp.sum(hi.reshape(16, 8, 256), axis=0)
        col_lo[:, pl.ds(c, 256)] += jnp.sum(lo.reshape(16, 8, 256), axis=0)

    def strips(first, last, groups):
        for g in groups:
            @pl.loop(first, last)
            def _(i):
                strip(i, g)

    def need_group(g):
        for slot in PLANE[4 * g : 4 * g + 4]:
            need_text(slot, 0)
            need_text(slot, 1)

    for d in NEAR:
        pairs[d].wait_recv()
    need_group(0)
    strips(0, 5, [0])
    need_group(1)
    strips(0, 5, [1])
    for d in FAR:
        send_pair(d)
    need_group(2)
    strips(0, 5, [2])
    for d in FAR:
        pairs[d].wait_recv()
    strips(5, 8, [0, 1, 2])
    need_group(3)
    strips(0, 8, [3])

    def log_of(hi, lo):
        return jnp.where(
            hi >= math.exp(-30.0), jnp.log(hi) + 30.0, jnp.log(lo) - 30.0
        )

    row_hi = jnp.sum(row_part[0].T, axis=0, keepdims=True)
    row_lo = jnp.sum(row_part[1].T, axis=0, keepdims=True)
    row_stat[0, :, :1024] = log_of(row_hi, row_lo)
    same = img[0].astype(f32) * txt[0].astype(f32)
    positive = scale * jnp.sum(same)
    row_stat[0, :, 1024:] = jnp.full((1, 128), positive, f32)
    for d in (4, 3, 5, 2, 6, 1, 7, 0):
        for k in range(2):
            if k or d:
                b = ISLOT[k, (8 - d) % 8]
                go(copy(row_stat.at[0], row_stat.at[b], rstat_s.at[b], rstat_r.at[b], at_line(k, d)))
    col_stat[0] = log_of(
        jnp.sum(col_hi[...], axis=0, keepdims=True), jnp.sum(col_lo[...], axis=0, keepdims=True)
    )
    for dy, dx in reversed(PLANE[1:]):
        b = TSLOT[(4 - dy) % 4, (4 - dx) % 4]
        go(copy(col_stat.at[0], col_stat.at[b], cstat_s.at[b], cstat_r.at[b], at_plane(dy, dx)))
    for j in range(1, 16):
        copy(row_stat.at[j], row_stat.at[j], rstat_s.at[j], rstat_r.at[j], at_line(0, 1)).wait_recv()
    for j in range(1, 16):
        copy(col_stat.at[j], col_stat.at[j], cstat_s.at[j], cstat_r.at[j], at_plane(0, 1)).wait_recv()

    def row_order(j):
        k, d = LINE[j]
        parts = row_stat[j, :, :1024]
        pieces = [None] * 16
        for p, (k2, d2) in enumerate(LINE):
            pieces[ISLOT[(k + k2) % 2, (d + d2) % 8]] = parts[:, p * n : p * n + n]
        return jnp.concatenate(pieces, axis=1)

    def col_order(j):
        dy, dx = PLANE[j]
        parts = col_stat[j]
        pieces = [None] * 16
        for p, (y2, x2) in enumerate(PLANE):
            pieces[TSLOT[(dy + y2) % 4, (dx + x2) % 4]] = parts[:, p * n : p * n + n]
        return jnp.concatenate(pieces, axis=1)

    def merged(parts):
        summit = functools.reduce(jnp.maximum, parts)
        total = sum(jnp.exp(p - summit) for p in parts)
        return summit + jnp.log(total)

    row_lse = merged([row_order(j) for j in range(16)])
    col_lse = merged([col_order(j) for j in range(16)])

    root = math.sqrt(0.5)
    row_factor = jnp.exp(row_lse * -0.5) * root
    col_factor = jnp.exp(col_lse * -0.5) * root
    row_scale[...] = jnp.broadcast_to(row_factor, (128, 1024)).T

    def weigh(i, carry):
        r = pl.multiple_of(i * 64, 64)
        a = row_scale[pl.ds(r, 64), :]
        for q in range(8):
            f = half[pl.ds(r, 64), q * 128 : q * 128 + 128]
            by_row = f * a
            by_col = f * col_factor[:, q * 128 : q * 128 + 128]
            weights[pl.ds(r, 64), q * 128 : q * 128 + 128] = (
                by_row * by_row + by_col * by_col
            ).astype(bf16)
        return carry

    lax.fori_loop(0, 16, weigh, 0)

    texts = txt[...].reshape(1024, 512)
    images = img[...].reshape(1024, 512)

    def image_share(first, last):
        return jnp.dot(
            weights[first * n : last * n, :], texts, preferred_element_type=f32
        ).reshape(last - first, n, 512)

    def send_share(h, first, last, to):
        img_out[first:last] = image_share(first, last).astype(bf16)
        count = last - first
        c = copy(
            img_out.at[pl.ds(first, count)], img_pair.at[pl.ds(to, count)],
            pg_s.at[h], pg_r.at[h], at_line(1, 0),
        )
        go(c)
        return c

    def text_shares(g):
        part = lax.dot_general(
            weights[:, g * 256 : g * 256 + 256], images, TN, preferred_element_type=f32
        ).reshape(4, n, 512)
        txt_out[4 * g : 4 * g + 4] = part.astype(bf16)
        for slot in PLANE[4 * g : 4 * g + 4]:
            dy, dx = slot
            j = TSLOT[slot]
            if dy:
                b = TSLOT[(4 - dy) % 4, dx]
                go(copy(
                    txt_out.at[j, rows(0)], txt_mid.at[b, rows(0)],
                    tm_s.at[2 * b], tm_r.at[2 * b], at_plane(dy, 0),
                ))
            if dx:
                b = TSLOT[dy, (4 - dx) % 4]
                go(copy(
                    txt_out.at[j, rows(1)], txt_mid.at[b, rows(1)],
                    tm_s.at[2 * b + 1], tm_r.at[2 * b + 1], at_plane(0, dx),
                ))

    far = send_share(0, 13, 16, 5)
    text_shares(3)
    near = send_share(1, 5, 10, 0)
    part = image_share(10, 13)
    far.wait_recv()
    img_out[10:13] = (part + img_pair[5:8].astype(f32)).astype(bf16)
    mids = []

    def send_mid(j, slot, h, to):
        c = copy(
            img_out.at[slot, rows(h)], img_mid.at[j, rows(h)],
            im_s.at[2 * j + h], im_r.at[2 * j + h], at_line(0, to),
        )
        go(c)
        mids.append(c)

    for h in range(2):
        send_mid(0, 10, h, 1)
        send_mid(1, 11, h, 7)
        send_mid(2, 12, h, (2, 6)[h])
    text_shares(2)
    part = image_share(0, 5)
    near.wait_recv()
    part = part + img_pair[0:5].astype(f32)
    img_own[...] = part[0]
    img_hold[...] = part[1:3]
    img_out[3:5] = part[3:5].astype(bf16)
    last = []
    for j, d in ((0, 1), (1, 7)):
        c = copy(img_out.at[3 + j], img_in.at[j], ig_s.at[j], ig_r.at[j], at_line(0, d))
        go(c)
        last.append(c)
    text_shares(1)
    text_shares(0)

    all_positive = sum(row_stat[j, :, 1024:] for j in range(16))
    row_loss[0] = jnp.full((1, 128), jnp.sum(row_lse), f32) - 2.0 * all_positive
    col_loss[0] = jnp.full((1, 128), jnp.sum(col_lse), f32)
    for dy, dx in PLANE[1:]:
        b = TSLOT[(4 - dy) % 4, (4 - dx) % 4]
        go(copy(row_loss.at[0], row_loss.at[b], rloss_s.at[b], rloss_r.at[b], at_plane(dy, dx)))
    for k, d in LINE[1:]:
        b = ISLOT[k, (8 - d) % 8]
        go(copy(col_loss.at[0], col_loss.at[b], closs_s.at[b], closs_r.at[b], at_line(k, d)))

    for c in mids:
        c.wait_recv()

    def mid(j, h):
        return img_mid[j, 32 * h : 32 * h + 32, :].astype(f32)

    for h in range(2):
        for j, d in ((0, 2), (1, 6)):
            total = img_hold[j, 32 * h : 32 * h + 32, :] + mid(j, h)
            if h == j:
                total = total + mid(2, h)
            img_send[j, 32 * h : 32 * h + 32, :] = total.astype(bf16)
            m = 2 + 2 * j + h
            c = copy(
                img_send.at[j, rows(h)], img_in.at[2 + j, rows(h)], ig_s.at[m], ig_r.at[m], at_line(0, d)
            )
            go(c)
            last.append(c)

    def need_mid(slot, h):
        m = 2 * TSLOT[slot] + h
        part = txt_mid.at[TSLOT[slot], rows(h)]
        copy(part, part, tm_s.at[m], tm_r.at[m], at_plane(0, 1)).wait_recv()

    def text_sum(d, h):
        slots = [(e, d) if h == 0 else (d, e) for e in range(4)]
        total = txt_out[TSLOT[slots[0]], 32 * h : 32 * h + 32, :].astype(f32)
        for slot in slots[1:]:
            need_mid(slot, h)
            total = total + txt_mid[TSLOT[slot], 32 * h : 32 * h + 32, :].astype(f32)
        return total

    ends = []
    for d in ROUND:
        for h in range(2):
            txt_send[d, 32 * h : 32 * h + 32, :] = text_sum(d, h).astype(bf16)
            m = 2 * (4 - d) + h
            c = copy(
                txt_send.at[d, rows(h)], txt_in.at[4 - d, rows(h)],
                tg_s.at[m], tg_r.at[m], at_plane(*((0, d) if h == 0 else (d, 0))),
            )
            go(c)
            ends.append(c)
    txt_total = jnp.concatenate([text_sum(0, 0), text_sum(0, 1)], axis=0)

    def finish(total, other, raw):
        unit, length = normal(raw)
        gradient = scale * total - scale * other.astype(f32)
        return (gradient - unit * jnp.sum(unit * gradient, axis=1, keepdims=True)) / length

    for j in range(1, 16):
        copy(row_loss.at[j], row_loss.at[j], rloss_s.at[j], rloss_r.at[j], at_line(0, 1)).wait_recv()
        copy(col_loss.at[j], col_loss.at[j], closs_s.at[j], closs_r.at[j], at_line(0, 1)).wait_recv()
    total = sum(row_loss[j] + col_loss[j] for j in range(16))
    loss_ref[...] = total / (2.0 * batch)
    for c in last:
        c.wait_recv()
    img_total = img_own[...]
    for j in range(4):
        img_total = img_total + img_in[j].astype(f32)
    img_grad_ref[...] = finish(img_total, txt[0], raw_img)
    for c in ends:
        c.wait_recv()
    for d in range(1, 4):
        txt_total = txt_total + txt_in[d].astype(f32)
    txt_grad_ref[...] = finish(txt_total, img[0], raw_txt)
    for c in sends:
        c.wait_send()


def write_out(loss_in, img_in, txt_in, loss_out, img_out, txt_out, sems):
    moves = [
        pltpu.make_async_copy(img_in, img_out, sems.at[0]),
        pltpu.make_async_copy(txt_in, txt_out, sems.at[1]),
    ]
    for c in moves:
        c.start()
    loss_out[...] = loss_in[0, :1]
    for c in moves:
        c.wait()


def on_device(image, text, logit_scale):
    batch = image.shape[0] * 256
    f32, bf16 = jnp.float32, jnp.bfloat16
    dma = pltpu.SemaphoreType.DMA
    vmem = pltpu.VMEM
    hbm = pl.BlockSpec(memory_space=pltpu.HBM)
    local = pl.BlockSpec(memory_space=vmem)
    loss, img_grad, txt_grad = pl.pallas_call(
        functools.partial(kernel, batch),
        out_shape=(
            jax.ShapeDtypeStruct((1, 128), f32),
            jax.ShapeDtypeStruct((64, 512), f32),
            jax.ShapeDtypeStruct((64, 512), f32),
        ),
        in_specs=[hbm, hbm, hbm],
        out_specs=[local] * 3,
        scratch_shapes=[
            vmem((64, 512), bf16),
            vmem((64, 512), bf16),
            pltpu.SMEM((1,), f32),
            vmem((16, 64, 512), bf16),
            vmem((16, 64, 512), bf16),
            vmem((1024, 1024), f32),
            vmem((1024, 1024), bf16),
            vmem((2, 1024, 128), f32),
            vmem((1024, 128), f32),
            vmem((8, 1024), f32),
            vmem((8, 1024), f32),
            vmem((16, 1, 1152), f32),
            vmem((16, 1, 1024), f32),
            vmem((16, 1, 128), f32),
            vmem((16, 1, 128), f32),
            vmem((16, 64, 512), bf16),
            vmem((8, 64, 512), bf16),
            vmem((2, 64, 512), f32),
            vmem((3, 64, 512), bf16),
            vmem((2, 64, 512), bf16),
            vmem((4, 64, 512), bf16),
            vmem((64, 512), f32),
            vmem((16, 64, 512), bf16),
            vmem((16, 64, 512), bf16),
            vmem((4, 64, 512), bf16),
            vmem((4, 64, 512), bf16),
            dma((3,)), dma((32,)), dma((32,)), dma((16,)), dma((16,)), dma((8,)), dma((8,)),
            dma((16,)), dma((16,)), dma((16,)), dma((16,)), dma((16,)), dma((16,)), dma((16,)), dma((16,)),
            dma((2,)), dma((2,)), dma((6,)), dma((6,)), dma((6,)), dma((6,)),
            dma((32,)), dma((32,)), dma((8,)), dma((8,)),
        ],
        compiler_params=pltpu.CompilerParams(
            collective_id=0, has_side_effects=True, vmem_limit_bytes=56 * 2**20
        ),
        cost_estimate=pl.CostEstimate(
            flops=6 * 1024 * 1024 * 512, bytes_accessed=400000, transcendentals=1024 * 1024
        ),
        name="contrast",
    )(image, text, logit_scale)
    return pl.pallas_call(
        write_out,
        out_shape=(
            jax.ShapeDtypeStruct((1,), f32),
            jax.ShapeDtypeStruct((64, 512), f32),
            jax.ShapeDtypeStruct((64, 512), f32),
        ),
        in_specs=[local, hbm, hbm],
        out_specs=[local, hbm, hbm],
        scratch_shapes=[dma((2,))],
        name="write_out",
    )(loss, img_grad, txt_grad)


def solution(mesh):
    torus = Mesh(mesh.devices.reshape(8, 4, 4, 2), AXES)
    return jax.shard_map(
        on_device,
        mesh=torus,
        in_specs=(P(AXES, None), P(AXES, None), P()),
        out_specs=(P(), P(AXES, None), P(AXES, None)),
        check_vma=False,
    )
```

time: 64.6 us -> 61.6 us (0.954)
  local copies, waits for them, and re-layouts: 2.93 us -> 0 us
  between operations: 2.47 us -> 1.28 us
  Pallas kernels: 59.1 us -> 60.1 us
    pallas_call x0 -> x1, Pallas kernels: none -> 10.2 us  [on_device(): pl.pallas_call(write_out, out_shape=(jax.ShapeDtypeStruct((1,), f32), jax...]
    pallas_call x1, Pallas kernels: 59.1 us -> 49.9 us  [on_device(): pl.pallas_call(functools.partial(kernel, batch), out_shape=(jax.ShapeDtyp...]
    unnamed x6 -> x0, local copies, waits for them, and re-layouts: 2.93 us -> none
where the time goes in v2:
time: 61.6 us; the launch traced here: 61.4 us
  Pallas kernels  60.1 us (98%)
  between operations  1.28 us (2%)
    pallas_call x1, Pallas kernels, on_device(): pl.pallas_call(functools.partial(kernel, batch), out_shape=(jax.ShapeDtyp...  49.9 us
    pallas_call x1, Pallas kernels, on_device(): pl.pallas_call(write_out, out_shape=(jax.ShapeDtypeStruct((1,), f32), jax...  10.2 us

profile of v2, /device:TPU:1, one launch (start us, length us, event | category | flops | bytes accessed | tf_op | source)
XLA Modules:
  0.0 61.4 jit_solution(13216337205794926082)
XLA Ops:
  1.3 49.9 %contrast.1 = (f32[1,128]{1,0:T(1,128)}, f32[64,512]{1,0:T(8,128)}, f32[64,512]{1,0:T(8,128)}) custom-call(bf16[64,512]{1,0:T(8,128)(2,1)} %image_ref.1, bf16[64,512]{1,0:T(8,128)(2,1)} %text_ref.1, f32[1]{0:T(128)S(6)} %copy.6.scale_ref), custom_call_target="tpu_custom_call" | custom-call | flops 3221225472 | bytes 400000 | tf_op jit(solution)/shard_map/contrast/pallas_call | solution.py:471
  51.2 10.2 %write_out.1 = (f32[1]{0:T(128)}, f32[64,512]{1,0:T(8,128)}, f32[64,512]{1,0:T(8,128)}) custom-call(f32[1,128]{1,0:T(1,128)} %get-tuple-element.6.loss_in, f32[64,512]{1,0:T(8,128)} %get-tuple-element.7.img_in, f32[64,512]{1,0:T(8,128)} %get-tuple-element.8.txt_in), custom_call_target="tpu_custom_call" | custom-call | tf_op jit(solution)/shard_map/write_out/pallas_call | solution.py:520

commit v3 on v2

--- a/solution.py
+++ b/solution.py
@@ -181,28 +181,27 @@
     power = scale * (0.5 * math.log2(math.e))
     down, up = math.exp(-15.0), math.exp(15.0)
 
-    def strip(i, g):
-        r = pl.multiple_of(i * 128, 128)
+    def strips(first, last, g):
         c = pl.multiple_of(g * 256, 256)
-        left = img[pl.ds(2 * i, 2)].reshape(128, 512)
         right = txt[pl.ds(4 * g, 4)].reshape(256, 512)
-        dots = lax.dot_general(left, right, NT, preferred_element_type=f32)
-        f = jnp.exp2(dots * power)
-        half[pl.ds(r, 128), pl.ds(c, 256)] = f
-        hi = f * down
-        hi = hi * hi
-        lo = jnp.minimum(f, 1.0) * up
-        lo = lo * lo
-        row_part[0, pl.ds(r, 128), :] += hi[:, :128] + hi[:, 128:]
-        row_part[1, pl.ds(r, 128), :] += lo[:, :128] + lo[:, 128:]
-        col_hi[:, pl.ds(c, 256)] += jnp.sum(hi.reshape(16, 8, 256), axis=0)
-        col_lo[:, pl.ds(c, 256)] += jnp.sum(lo.reshape(16, 8, 256), axis=0)
-
-    def strips(first, last, groups):
-        for g in groups:
-            @pl.loop(first, last)
-            def _(i):
-                strip(i, g)
+        hi_col = col_hi[:, pl.ds(c, 256)]
+        lo_col = col_lo[:, pl.ds(c, 256)]
+        for i in range(first, last):
+            r = 128 * i
+            left = img[2 * i : 2 * i + 2].reshape(128, 512)
+            dots = lax.dot_general(left, right, NT, preferred_element_type=f32)
+            f = jnp.exp2(dots * power)
+            half[r : r + 128, pl.ds(c, 256)] = f
+            hi = f * down
+            hi = hi * hi
+            lo = jnp.minimum(f, 1.0) * up
+            lo = lo * lo
+            row_part[0, r : r + 128, :] += hi[:, :128] + hi[:, 128:]
+            row_part[1, r : r + 128, :] += lo[:, :128] + lo[:, 128:]
+            hi_col = hi_col + jnp.sum(hi.reshape(16, 8, 256), axis=0)
+            lo_col = lo_col + jnp.sum(lo.reshape(16, 8, 256), axis=0)
+        col_hi[:, pl.ds(c, 256)] = hi_col
+        col_lo[:, pl.ds(c, 256)] = lo_col
 
     def need_group(g):
         for slot in PLANE[4 * g : 4 * g + 4]:
@@ -212,18 +211,22 @@
     for d in NEAR:
         pairs[d].wait_recv()
     need_group(0)
-    strips(0, 5, [0])
+    strips(0, 5, 0)
     need_group(1)
-    strips(0, 5, [1])
+    strips(0, 5, 1)
     for d in FAR:
         send_pair(d)
     need_group(2)
-    strips(0, 5, [2])
+    strips(0, 5, 2)
     for d in FAR:
         pairs[d].wait_recv()
-    strips(5, 8, [0, 1, 2])
+
+    @pl.loop(0, 3)
+    def _(g):
+        strips(5, 8, g)
+
     need_group(3)
-    strips(0, 8, [3])
+    strips(0, 8, 3)
 
     def log_of(hi, lo):
         return jnp.where(
@@ -449,16 +452,10 @@
         c.wait_send()
 
 
-def write_out(loss_in, img_in, txt_in, loss_out, img_out, txt_out, sems):
-    moves = [
-        pltpu.make_async_copy(img_in, img_out, sems.at[0]),
-        pltpu.make_async_copy(txt_in, txt_out, sems.at[1]),
-    ]
-    for c in moves:
-        c.start()
+def write_out(loss_in, img_in, txt_in, loss_out, img_out, txt_out):
     loss_out[...] = loss_in[0, :1]
-    for c in moves:
-        c.wait()
+    img_out[...] = img_in[...]
+    txt_out[...] = txt_in[...]
 
 
 def on_device(image, text, logit_scale):
@@ -524,9 +521,8 @@
             jax.ShapeDtypeStruct((64, 512), f32),
             jax.ShapeDtypeStruct((64, 512), f32),
         ),
-        in_specs=[local, hbm, hbm],
-        out_specs=[local, hbm, hbm],
-        scratch_shapes=[dma((2,))],
+        in_specs=[local] * 3,
+        out_specs=[local] * 3,
         name="write_out",
     )(loss, img_grad, txt_grad)
 

time: 61.6 us -> 49.5 us (0.80)
  Pallas kernels: 60.1 us -> 48.1 us
    pallas_call x1, Pallas kernels: 10.2 us -> 1.69 us  [on_device(): pl.pallas_call(write_out, out_shape=(jax.ShapeDtypeStruct((1,), f32), jax...]
    pallas_call x1, Pallas kernels: 49.9 us -> 46.4 us  [on_device(): pl.pallas_call(functools.partial(kernel, batch), out_shape=(jax.ShapeDtyp...]
where the time goes in v3:
time: 49.5 us; the launch traced here: 49.4 us
  Pallas kernels  48.1 us (97%)
  between operations  1.28 us (3%)
    pallas_call x1, Pallas kernels, on_device(): pl.pallas_call(functools.partial(kernel, batch), out_shape=(jax.ShapeDtyp...  46.4 us
    pallas_call x1, Pallas kernels, on_device(): pl.pallas_call(write_out, out_shape=(jax.ShapeDtypeStruct((1,), f32), jax...  1.69 us

profile of v3, /device:TPU:1, one launch (start us, length us, event | category | flops | bytes accessed | tf_op | source)
XLA Modules:
  0.0 49.4 jit_solution(9158834677806502079)
XLA Ops:
  1.3 46.4 %contrast.1 = (f32[1,128]{1,0:T(1,128)}, f32[64,512]{1,0:T(8,128)}, f32[64,512]{1,0:T(8,128)}) custom-call(bf16[64,512]{1,0:T(8,128)(2,1)} %image_ref.1, bf16[64,512]{1,0:T(8,128)(2,1)} %text_ref.1, f32[1]{0:T(128)S(6)} %copy.6.scale_ref), custom_call_target="tpu_custom_call" | custom-call | flops 3221225472 | bytes 400000 | tf_op jit(solution)/shard_map/contrast/pallas_call | solution.py:468
  47.7 1.7 %write_out.1 = (f32[1]{0:T(128)}, f32[64,512]{1,0:T(8,128)}, f32[64,512]{1,0:T(8,128)}) custom-call(f32[1,128]{1,0:T(1,128)} %get-tuple-element.6.loss_in, f32[64,512]{1,0:T(8,128)} %get-tuple-element.7.img_in, f32[64,512]{1,0:T(8,128)} %get-tuple-element.8.txt_in), custom_call_target="tpu_custom_call" | custom-call | tf_op jit(solution)/shard_map/write_out/pallas_call | solution.py:517

commit v4 on v3

--- a/solution.py
+++ b/solution.py
@@ -48,9 +48,7 @@
     row_stat, col_stat, row_loss, col_loss,
     img_out, img_pair, img_hold, img_mid, img_send, img_in, img_own,
     txt_out, txt_mid, txt_send, txt_in,
-    load, txt_s, txt_r, img_s, img_r, pair_s, pair_r,
-    rstat_s, rstat_r, cstat_s, cstat_r, rloss_s, rloss_r, closs_s, closs_r,
-    pg_s, pg_r, im_s, im_r, ig_s, ig_r, tm_s, tm_r, tg_s, tg_r,
+    load, sent, txt_r, img_r, pair_r, stat_r, pg_r, im_r, ig_r, tm_r, tg_r,
 ):
     n = 64
     f32, bf16 = jnp.float32, jnp.bfloat16
@@ -88,62 +86,57 @@
     txt[0] = normal(raw_txt)[0].astype(bf16)
     pl.semaphore_wait(barrier, 30)
 
-    sends = []
+    TXT, IMG, PAIR, RSTAT, CSTAT, RLOSS, CLOSS, SHARE, MID, LAST, TMID, END = range(12)
 
     def rows(h):
         return pl.ds(32 * h, 32)
 
-    def go(c):
-        c.start()
-        sends.append(c)
-
-    def text_part(slot, h):
-        j = TSLOT[slot]
-        return txt.at[j, rows(h)], txt_s.at[2 * j + h], txt_r.at[2 * j + h]
+    def take(ref, sem):
+        copy(ref, ref, sent.at[0], sem, at_line(1, 0)).wait_recv()
+
+    def drain(ref, kind):
+        copy(ref, ref, sent.at[kind], pair_r.at[0], at_line(1, 0)).wait_send()
+
+    first_hop = [((0, d), 0) for d in (1, 2, 3)] + [((d, 0), 1) for d in (1, 2, 3)]
+
+    def text_sem(slot, h):
+        if (slot, h) in first_hop:
+            return txt_r.at[first_hop.index((slot, h))]
+        return txt_r.at[6 + TSLOT[slot] // 4]
 
     def send_text(source, h, dy, dx):
         landing = ((source[0] - dy) % 4, (source[1] - dx) % 4)
-        dst, s, r = text_part(landing, h)
-        go(copy(text_part(source, h)[0], dst, s, r, at_plane(dy, dx)))
-
-    def image_part(d, h):
-        return img.at[ISLOT[0, d], rows(h)], img_s.at[2 * d + h], img_r.at[2 * d + h]
+        copy(
+            txt.at[TSLOT[source], rows(h)], txt.at[TSLOT[landing], rows(h)],
+            sent.at[TXT], text_sem(landing, h), at_plane(dy, dx),
+        ).start()
+
+    def image_sem(d, h):
+        return img_r.at[{2: h, 6: 2 + h, 1: 4, 7: 5, 3: 6, 5: 7, 4: 8}[d]]
 
     def send_image(source, h, d):
-        dst, s, r = image_part((source - d) % 8, h)
-        go(copy(image_part(source, h)[0], dst, s, r, at_line(0, d)))
-
-    arrived = set()
-
-    def need_text(slot, h):
-        if slot != (0, 0) and (slot, h) not in arrived:
-            arrived.add((slot, h))
-            part, s, r = text_part(slot, h)
-            copy(part, part, s, r, at_plane(0, 1)).wait_recv()
-
-    def need_image(d, h):
-        if d and (d, h) not in arrived:
-            arrived.add((d, h))
-            part, s, r = image_part(d, h)
-            copy(part, part, s, r, at_line(0, 1)).wait_recv()
-
-    pairs = {}
+        landing = (source - d) % 8
+        copy(
+            img.at[ISLOT[0, source], rows(h)], img.at[ISLOT[0, landing], rows(h)],
+            sent.at[IMG], image_sem(landing, h), at_line(0, d),
+        ).start()
 
     def send_pair(d):
-        need_image(d, 0)
-        need_image(d, 1)
-        pairs[d] = copy(
-            img.at[ISLOT[0, d]], img.at[ISLOT[1, d]], pair_s.at[d], pair_r.at[d], at_line(1, 0)
-        )
-        go(pairs[d])
+        if d in (1, 7, 3, 5, 4):
+            take(img.at[ISLOT[0, d]], image_sem(d, 0))
+        copy(
+            img.at[ISLOT[0, d]], img.at[ISLOT[1, d]],
+            sent.at[PAIR], pair_r.at[int(d in FAR)], at_line(1, 0),
+        ).start()
 
     def spread(source, h):
-        need_text(source, h)
+        if (source, h) in first_hop:
+            take(txt.at[TSLOT[source], rows(h)], text_sem(source, h))
         for d in ROUND:
             send_text(source, h, *((d, 0) if h == 0 else (0, d)))
 
     def relay(source, h):
-        need_image(source, h)
+        take(img.at[ISLOT[0, source], rows(h)], image_sem(source, h))
         if source == 6:
             if h == 0:
                 send_image(6, 0, 2)
@@ -155,26 +148,26 @@
 
     send_image(0, 0, 2)
     send_image(0, 0, 6)
-    for d in ROUND:
+    send_image(0, 1, 2)
+    send_image(0, 1, 6)
+    for d in (1, 3, 2):
         send_text((0, 0), 0, 0, d)
         send_text((0, 0), 1, d, 0)
-    send_image(0, 1, 2)
-    send_image(0, 1, 6)
-    spread((0, 0), 0)
-    spread((0, 0), 1)
     for h in range(2):
         send_image(0, h, 1)
         send_image(0, h, 7)
+    spread((0, 0), 0)
+    spread((0, 0), 1)
     send_pair(0)
+    relay(6, 0)
+    relay(2, 0)
     for d in (3, 1):
         spread((0, d), 0)
         spread((d, 0), 1)
-    relay(6, 0)
-    relay(2, 0)
+    relay(6, 1)
+    relay(2, 1)
     spread((0, 2), 0)
     spread((2, 0), 1)
-    relay(6, 1)
-    relay(2, 1)
     for d in (2, 6, 1, 7):
         send_pair(d)
 
@@ -204,29 +197,30 @@
         col_lo[:, pl.ds(c, 256)] = lo_col
 
     def need_group(g):
-        for slot in PLANE[4 * g : 4 * g + 4]:
-            need_text(slot, 0)
-            need_text(slot, 1)
-
-    for d in NEAR:
-        pairs[d].wait_recv()
+        count = 8 - sum(TSLOT[slot] // 4 == g for slot, _ in first_hop) - 2 * (g == 0)
+        take(img.at[pl.ds(0, count), rows(0)], txt_r.at[6 + g])
+
+    take(img.at[pl.ds(0, 5)], pair_r.at[0])
     need_group(0)
     strips(0, 5, 0)
     need_group(1)
     strips(0, 5, 1)
-    for d in FAR:
-        send_pair(d)
     need_group(2)
     strips(0, 5, 2)
     for d in FAR:
-        pairs[d].wait_recv()
-
-    @pl.loop(0, 3)
+        send_pair(d)
+    need_group(3)
+    strips(0, 5, 3)
+
+    @pl.loop(0, 4)
     def _(g):
-        strips(5, 8, g)
-
-    need_group(3)
-    strips(0, 8, 3)
+        strips(5, 6, g)
+
+    take(img.at[pl.ds(0, 3)], pair_r.at[1])
+
+    @pl.loop(0, 4)
+    def _(g):
+        strips(6, 8, g)
 
     def log_of(hi, lo):
         return jnp.where(
@@ -243,17 +237,15 @@
         for k in range(2):
             if k or d:
                 b = ISLOT[k, (8 - d) % 8]
-                go(copy(row_stat.at[0], row_stat.at[b], rstat_s.at[b], rstat_r.at[b], at_line(k, d)))
+                copy(row_stat.at[0], row_stat.at[b], sent.at[RSTAT], stat_r.at[0], at_line(k, d)).start()
     col_stat[0] = log_of(
         jnp.sum(col_hi[...], axis=0, keepdims=True), jnp.sum(col_lo[...], axis=0, keepdims=True)
     )
     for dy, dx in reversed(PLANE[1:]):
         b = TSLOT[(4 - dy) % 4, (4 - dx) % 4]
-        go(copy(col_stat.at[0], col_stat.at[b], cstat_s.at[b], cstat_r.at[b], at_plane(dy, dx)))
-    for j in range(1, 16):
-        copy(row_stat.at[j], row_stat.at[j], rstat_s.at[j], rstat_r.at[j], at_line(0, 1)).wait_recv()
-    for j in range(1, 16):
-        copy(col_stat.at[j], col_stat.at[j], cstat_s.at[j], cstat_r.at[j], at_plane(0, 1)).wait_recv()
+        copy(col_stat.at[0], col_stat.at[b], sent.at[CSTAT], stat_r.at[1], at_plane(dy, dx)).start()
+    take(row_stat.at[pl.ds(1, 15)], stat_r.at[0])
+    take(col_stat.at[pl.ds(1, 15)], stat_r.at[1])
 
     def row_order(j):
         k, d = LINE[j]
@@ -284,19 +276,14 @@
     col_factor = jnp.exp(col_lse * -0.5) * root
     row_scale[...] = jnp.broadcast_to(row_factor, (128, 1024)).T
 
-    def weigh(i, carry):
-        r = pl.multiple_of(i * 64, 64)
-        a = row_scale[pl.ds(r, 64), :]
-        for q in range(8):
-            f = half[pl.ds(r, 64), q * 128 : q * 128 + 128]
-            by_row = f * a
-            by_col = f * col_factor[:, q * 128 : q * 128 + 128]
-            weights[pl.ds(r, 64), q * 128 : q * 128 + 128] = (
-                by_row * by_row + by_col * by_col
-            ).astype(bf16)
-        return carry
-
-    lax.fori_loop(0, 16, weigh, 0)
+    def weigh(first, last):
+        for r in range(64 * first, 64 * last, 64):
+            a = row_scale[r : r + 64, :]
+            for q in range(0, 1024, 128):
+                f = half[r : r + 64, q : q + 128]
+                by_row = f * a
+                by_col = f * col_factor[:, q : q + 128]
+                weights[r : r + 64, q : q + 128] = (by_row * by_row + by_col * by_col).astype(bf16)
 
     texts = txt[...].reshape(1024, 512)
     images = img[...].reshape(1024, 512)
@@ -309,12 +296,10 @@
     def send_share(h, first, last, to):
         img_out[first:last] = image_share(first, last).astype(bf16)
         count = last - first
-        c = copy(
+        copy(
             img_out.at[pl.ds(first, count)], img_pair.at[pl.ds(to, count)],
-            pg_s.at[h], pg_r.at[h], at_line(1, 0),
-        )
-        go(c)
-        return c
+            sent.at[SHARE], pg_r.at[h], at_line(1, 0),
+        ).start()
 
     def text_shares(g):
         part = lax.dot_general(
@@ -326,49 +311,46 @@
             j = TSLOT[slot]
             if dy:
                 b = TSLOT[(4 - dy) % 4, dx]
-                go(copy(
+                copy(
                     txt_out.at[j, rows(0)], txt_mid.at[b, rows(0)],
-                    tm_s.at[2 * b], tm_r.at[2 * b], at_plane(dy, 0),
-                ))
+                    sent.at[TMID], tm_r.at[2 * dx], at_plane(dy, 0),
+                ).start()
             if dx:
                 b = TSLOT[dy, (4 - dx) % 4]
-                go(copy(
+                copy(
                     txt_out.at[j, rows(1)], txt_mid.at[b, rows(1)],
-                    tm_s.at[2 * b + 1], tm_r.at[2 * b + 1], at_plane(0, dx),
-                ))
-
-    far = send_share(0, 13, 16, 5)
-    text_shares(3)
-    near = send_share(1, 5, 10, 0)
+                    sent.at[TMID], tm_r.at[2 * dy + 1], at_plane(0, dx),
+                ).start()
+
+    def send_mid(j, slot, h, to):
+        copy(
+            img_out.at[slot, rows(h)], img_mid.at[j, rows(h)],
+            sent.at[MID], im_r.at[h], at_line(0, to),
+        ).start()
+
+    weigh(13, 16)
+    send_share(0, 13, 16, 5)
+    weigh(10, 13)
     part = image_share(10, 13)
-    far.wait_recv()
+    weigh(5, 10)
+    take(img_pair.at[pl.ds(5, 3)], pg_r.at[0])
     img_out[10:13] = (part + img_pair[5:8].astype(f32)).astype(bf16)
-    mids = []
-
-    def send_mid(j, slot, h, to):
-        c = copy(
-            img_out.at[slot, rows(h)], img_mid.at[j, rows(h)],
-            im_s.at[2 * j + h], im_r.at[2 * j + h], at_line(0, to),
-        )
-        go(c)
-        mids.append(c)
-
     for h in range(2):
         send_mid(0, 10, h, 1)
         send_mid(1, 11, h, 7)
         send_mid(2, 12, h, (2, 6)[h])
-    text_shares(2)
+    send_share(1, 5, 10, 0)
+    weigh(0, 5)
+    text_shares(3)
     part = image_share(0, 5)
-    near.wait_recv()
+    take(img_pair.at[pl.ds(0, 5)], pg_r.at[1])
     part = part + img_pair[0:5].astype(f32)
     img_own[...] = part[0]
     img_hold[...] = part[1:3]
     img_out[3:5] = part[3:5].astype(bf16)
-    last = []
     for j, d in ((0, 1), (1, 7)):
-        c = copy(img_out.at[3 + j], img_in.at[j], ig_s.at[j], ig_r.at[j], at_line(0, d))
-        go(c)
-        last.append(c)
+        copy(img_out.at[3 + j], img_in.at[j], sent.at[LAST], ig_r.at[0], at_line(0, d)).start()
+    text_shares(2)
     text_shares(1)
     text_shares(0)
 
@@ -377,54 +359,41 @@
     col_loss[0] = jnp.full((1, 128), jnp.sum(col_lse), f32)
     for dy, dx in PLANE[1:]:
         b = TSLOT[(4 - dy) % 4, (4 - dx) % 4]
-        go(copy(row_loss.at[0], row_loss.at[b], rloss_s.at[b], rloss_r.at[b], at_plane(dy, dx)))
+        copy(row_loss.at[0], row_loss.at[b], sent.at[RLOSS], stat_r.at[2], at_plane(dy, dx)).start()
     for k, d in LINE[1:]:
         b = ISLOT[k, (8 - d) % 8]
-        go(copy(col_loss.at[0], col_loss.at[b], closs_s.at[b], closs_r.at[b], at_line(k, d)))
-
-    for c in mids:
-        c.wait_recv()
+        copy(col_loss.at[0], col_loss.at[b], sent.at[CLOSS], stat_r.at[3], at_line(k, d)).start()
 
     def mid(j, h):
         return img_mid[j, 32 * h : 32 * h + 32, :].astype(f32)
 
     for h in range(2):
+        take(img_mid.at[pl.ds(0, 3), rows(h)], im_r.at[h])
         for j, d in ((0, 2), (1, 6)):
             total = img_hold[j, 32 * h : 32 * h + 32, :] + mid(j, h)
             if h == j:
                 total = total + mid(2, h)
             img_send[j, 32 * h : 32 * h + 32, :] = total.astype(bf16)
-            m = 2 + 2 * j + h
-            c = copy(
-                img_send.at[j, rows(h)], img_in.at[2 + j, rows(h)], ig_s.at[m], ig_r.at[m], at_line(0, d)
-            )
-            go(c)
-            last.append(c)
-
-    def need_mid(slot, h):
-        m = 2 * TSLOT[slot] + h
-        part = txt_mid.at[TSLOT[slot], rows(h)]
-        copy(part, part, tm_s.at[m], tm_r.at[m], at_plane(0, 1)).wait_recv()
+            copy(
+                img_send.at[j, rows(h)], img_in.at[2 + j, rows(h)],
+                sent.at[LAST], ig_r.at[0], at_line(0, d),
+            ).start()
 
     def text_sum(d, h):
         slots = [(e, d) if h == 0 else (d, e) for e in range(4)]
+        take(txt_mid.at[pl.ds(0, 3), rows(h)], tm_r.at[2 * d + h])
         total = txt_out[TSLOT[slots[0]], 32 * h : 32 * h + 32, :].astype(f32)
         for slot in slots[1:]:
-            need_mid(slot, h)
             total = total + txt_mid[TSLOT[slot], 32 * h : 32 * h + 32, :].astype(f32)
         return total
 
-    ends = []
     for d in ROUND:
         for h in range(2):
             txt_send[d, 32 * h : 32 * h + 32, :] = text_sum(d, h).astype(bf16)
-            m = 2 * (4 - d) + h
-            c = copy(
+            copy(
                 txt_send.at[d, rows(h)], txt_in.at[4 - d, rows(h)],
-                tg_s.at[m], tg_r.at[m], at_plane(*((0, d) if h == 0 else (d, 0))),
-            )
-            go(c)
-            ends.append(c)
+                sent.at[END], tg_r.at[0], at_plane(*((0, d) if h == 0 else (d, 0))),
+            ).start()
     txt_total = jnp.concatenate([text_sum(0, 0), text_sum(0, 1)], axis=0)
 
     def finish(total, other, raw):
@@ -432,24 +401,31 @@
         gradient = scale * total - scale * other.astype(f32)
         return (gradient - unit * jnp.sum(unit * gradient, axis=1, keepdims=True)) / length
 
-    for j in range(1, 16):
-        copy(row_loss.at[j], row_loss.at[j], rloss_s.at[j], rloss_r.at[j], at_line(0, 1)).wait_recv()
-        copy(col_loss.at[j], col_loss.at[j], closs_s.at[j], closs_r.at[j], at_line(0, 1)).wait_recv()
+    take(row_loss.at[pl.ds(1, 15)], stat_r.at[2])
+    take(col_loss.at[pl.ds(1, 15)], stat_r.at[3])
     total = sum(row_loss[j] + col_loss[j] for j in range(16))
     loss_ref[...] = total / (2.0 * batch)
-    for c in last:
-        c.wait_recv()
+    take(img_in, ig_r.at[0])
     img_total = img_own[...]
     for j in range(4):
         img_total = img_total + img_in[j].astype(f32)
     img_grad_ref[...] = finish(img_total, txt[0], raw_img)
-    for c in ends:
-        c.wait_recv()
+    take(txt_in.at[pl.ds(1, 3)], tg_r.at[0])
     for d in range(1, 4):
         txt_total = txt_total + txt_in[d].astype(f32)
     txt_grad_ref[...] = finish(txt_total, img[0], raw_txt)
-    for c in sends:
-        c.wait_send()
+    drain(txt.at[pl.ds(0, 15)], TXT)
+    drain(img.at[pl.ds(0, 7)], IMG)
+    drain(img.at[pl.ds(0, 8)], PAIR)
+    drain(row_stat.at[pl.ds(1, 15)], RSTAT)
+    drain(col_stat.at[pl.ds(1, 15)], CSTAT)
+    drain(row_loss.at[pl.ds(1, 15)], RLOSS)
+    drain(col_loss.at[pl.ds(1, 15)], CLOSS)
+    drain(img_pair, SHARE)
+    drain(img_mid, MID)
+    drain(img_in, LAST)
+    drain(txt.at[pl.ds(0, 12)], TMID)
+    drain(txt_in.at[pl.ds(1, 3)], END)
 
 
 def write_out(loss_in, img_in, txt_in, loss_out, img_out, txt_out):
@@ -501,10 +477,8 @@
             vmem((16, 64, 512), bf16),
             vmem((4, 64, 512), bf16),
             vmem((4, 64, 512), bf16),
-            dma((3,)), dma((32,)), dma((32,)), dma((16,)), dma((16,)), dma((8,)), dma((8,)),
-            dma((16,)), dma((16,)), dma((16,)), dma((16,)), dma((16,)), dma((16,)), dma((16,)), dma((16,)),
-            dma((2,)), dma((2,)), dma((6,)), dma((6,)), dma((6,)), dma((6,)),
-            dma((32,)), dma((32,)), dma((8,)), dma((8,)),
+            dma((3,)), dma((12,)), dma((10,)), dma((9,)), dma((2,)), dma((4,)), dma((2,)), dma((2,)),
+            dma((1,)), dma((8,)), dma((1,)),
         ],
         compiler_params=pltpu.CompilerParams(
             collective_id=0, has_side_effects=True, vmem_limit_bytes=56 * 2**20

time: 49.5 us -> 48.8 us (0.986)
  Pallas kernels: 48.1 us -> 47.3 us
    pallas_call x1, Pallas kernels: 46.4 us -> 45.7 us  [on_device(): pl.pallas_call(functools.partial(kernel, batch), out_shape=(jax.ShapeDtyp...]
where the time goes in v4:
time: 48.8 us; the launch traced here: 48.6 us
  Pallas kernels  47.3 us (97%)
  between operations  1.28 us (3%)
    pallas_call x1, Pallas kernels, on_device(): pl.pallas_call(functools.partial(kernel, batch), out_shape=(jax.ShapeDtyp...  45.7 us
    pallas_call x1, Pallas kernels, on_device(): pl.pallas_call(write_out, out_shape=(jax.ShapeDtypeStruct((1,), f32), jax...  1.69 us

profile of v4, /device:TPU:1, one launch (start us, length us, event | category | flops | bytes accessed | tf_op | source)
XLA Modules:
  0.0 48.6 jit_solution(17506912571478719026)
XLA Ops:
  1.3 45.7 %contrast.1 = (f32[1,128]{1,0:T(1,128)}, f32[64,512]{1,0:T(8,128)}, f32[64,512]{1,0:T(8,128)}) custom-call(bf16[64,512]{1,0:T(8,128)(2,1)} %image_ref.1, bf16[64,512]{1,0:T(8,128)(2,1)} %text_ref.1, f32[1]{0:T(128)S(6)} %copy.6.scale_ref), custom_call_target="tpu_custom_call" | custom-call | flops 3221225472 | bytes 400000 | tf_op jit(solution)/shard_map/contrast/pallas_call | solution.py:444
  46.9 1.7 %write_out.1 = (f32[1]{0:T(128)}, f32[64,512]{1,0:T(8,128)}, f32[64,512]{1,0:T(8,128)}) custom-call(f32[1,128]{1,0:T(1,128)} %get-tuple-element.6.loss_in, f32[64,512]{1,0:T(8,128)} %get-tuple-element.7.img_in, f32[64,512]{1,0:T(8,128)} %get-tuple-element.8.txt_in), custom_call_target="tpu_custom_call" | custom-call | tf_op jit(solution)/shard_map/write_out/pallas_call | solution.py:491

commit v5 on v4

--- a/solution.py
+++ b/solution.py
@@ -44,7 +44,7 @@
 
 def kernel(
     batch, image_ref, text_ref, scale_ref, loss_ref, img_grad_ref, txt_grad_ref,
-    raw_img, raw_txt, raw_scale, img, txt, half, weights, row_part, row_scale, col_hi, col_lo,
+    raw_img, raw_txt, raw_scale, unit, over_length, img, txt, half, weights, row_part, row_scale, col_hi, col_lo,
     row_stat, col_stat, row_loss, col_loss,
     img_out, img_pair, img_hold, img_mid, img_send, img_in, img_own,
     txt_out, txt_mid, txt_send, txt_in,
@@ -244,6 +244,9 @@
     for dy, dx in reversed(PLANE[1:]):
         b = TSLOT[(4 - dy) % 4, (4 - dx) % 4]
         copy(col_stat.at[0], col_stat.at[b], sent.at[CSTAT], stat_r.at[1], at_plane(dy, dx)).start()
+    for j, raw in enumerate((raw_img, raw_txt)):
+        unit[j], length = normal(raw)
+        over_length[j] = jnp.broadcast_to(1.0 / length, (n, 128))
     take(row_stat.at[pl.ds(1, 15)], stat_r.at[0])
     take(col_stat.at[pl.ds(1, 15)], stat_r.at[1])
 
@@ -330,30 +333,6 @@
 
     weigh(13, 16)
     send_share(0, 13, 16, 5)
-    weigh(10, 13)
-    part = image_share(10, 13)
-    weigh(5, 10)
-    take(img_pair.at[pl.ds(5, 3)], pg_r.at[0])
-    img_out[10:13] = (part + img_pair[5:8].astype(f32)).astype(bf16)
-    for h in range(2):
-        send_mid(0, 10, h, 1)
-        send_mid(1, 11, h, 7)
-        send_mid(2, 12, h, (2, 6)[h])
-    send_share(1, 5, 10, 0)
-    weigh(0, 5)
-    text_shares(3)
-    part = image_share(0, 5)
-    take(img_pair.at[pl.ds(0, 5)], pg_r.at[1])
-    part = part + img_pair[0:5].astype(f32)
-    img_own[...] = part[0]
-    img_hold[...] = part[1:3]
-    img_out[3:5] = part[3:5].astype(bf16)
-    for j, d in ((0, 1), (1, 7)):
-        copy(img_out.at[3 + j], img_in.at[j], sent.at[LAST], ig_r.at[0], at_line(0, d)).start()
-    text_shares(2)
-    text_shares(1)
-    text_shares(0)
-
     all_positive = sum(row_stat[j, :, 1024:] for j in range(16))
     row_loss[0] = jnp.full((1, 128), jnp.sum(row_lse), f32) - 2.0 * all_positive
     col_loss[0] = jnp.full((1, 128), jnp.sum(col_lse), f32)
@@ -363,6 +342,29 @@
     for k, d in LINE[1:]:
         b = ISLOT[k, (8 - d) % 8]
         copy(col_loss.at[0], col_loss.at[b], sent.at[CLOSS], stat_r.at[3], at_line(k, d)).start()
+    weigh(10, 13)
+    weigh(5, 10)
+    send_share(1, 5, 10, 0)
+    weigh(0, 5)
+    text_shares(3)
+    text_shares(2)
+    part = image_share(10, 13)
+    take(img_pair.at[pl.ds(5, 3)], pg_r.at[0])
+    img_out[10:13] = (part + img_pair[5:8].astype(f32)).astype(bf16)
+    for h in range(2):
+        send_mid(0, 10, h, 1)
+        send_mid(1, 11, h, 7)
+        send_mid(2, 12, h, (2, 6)[h])
+    text_shares(1)
+    text_shares(0)
+    part = image_share(0, 5)
+    take(img_pair.at[pl.ds(0, 5)], pg_r.at[1])
+    part = part + img_pair[0:5].astype(f32)
+    img_own[...] = part[0]
+    img_hold[...] = part[1:3]
+    img_out[3:5] = part[3:5].astype(bf16)
+    for j, d in ((0, 1), (1, 7)):
+        copy(img_out.at[3 + j], img_in.at[j], sent.at[LAST], ig_r.at[0], at_line(0, d)).start()
 
     def mid(j, h):
         return img_mid[j, 32 * h : 32 * h + 32, :].astype(f32)
@@ -396,10 +398,10 @@
             ).start()
     txt_total = jnp.concatenate([text_sum(0, 0), text_sum(0, 1)], axis=0)
 
-    def finish(total, other, raw):
-        unit, length = normal(raw)
+    def finish(j, total, other):
         gradient = scale * total - scale * other.astype(f32)
-        return (gradient - unit * jnp.sum(unit * gradient, axis=1, keepdims=True)) / length
+        inner = jnp.sum(unit[j] * gradient, axis=1, keepdims=True)
+        return (gradient - unit[j] * inner) * over_length[j, :, :1]
 
     take(row_loss.at[pl.ds(1, 15)], stat_r.at[2])
     take(col_loss.at[pl.ds(1, 15)], stat_r.at[3])
@@ -409,11 +411,11 @@
     img_total = img_own[...]
     for j in range(4):
         img_total = img_total + img_in[j].astype(f32)
-    img_grad_ref[...] = finish(img_total, txt[0], raw_img)
+    img_grad_ref[...] = finish(0, img_total, txt[0])
     take(txt_in.at[pl.ds(1, 3)], tg_r.at[0])
     for d in range(1, 4):
         txt_total = txt_total + txt_in[d].astype(f32)
-    txt_grad_ref[...] = finish(txt_total, img[0], raw_txt)
+    txt_grad_ref[...] = finish(1, txt_total, img[0])
     drain(txt.at[pl.ds(0, 15)], TXT)
     drain(img.at[pl.ds(0, 7)], IMG)
     drain(img.at[pl.ds(0, 8)], PAIR)
@@ -454,6 +456,8 @@
             vmem((64, 512), bf16),
             vmem((64, 512), bf16),
             pltpu.SMEM((1,), f32),
+            vmem((2, 64, 512), f32),
+            vmem((2, 64, 128), f32),
             vmem((16, 64, 512), bf16),
             vmem((16, 64, 512), bf16),
             vmem((1024, 1024), f32),

time: 48.8 us -> 46.5 us (0.953)
  Pallas kernels: 47.3 us -> 45.1 us
    pallas_call x1, Pallas kernels: 45.7 us -> 43.4 us  [on_device(): pl.pallas_call(functools.partial(kernel, batch), out_shape=(jax.ShapeDtyp...]
where the time goes in v5:
time: 46.5 us; the launch traced here: 46.3 us
  Pallas kernels  45.1 us (97%)
  between operations  1.28 us (3%)
    pallas_call x1, Pallas kernels, on_device(): pl.pallas_call(functools.partial(kernel, batch), out_shape=(jax.ShapeDtyp...  43.4 us
    pallas_call x1, Pallas kernels, on_device(): pl.pallas_call(write_out, out_shape=(jax.ShapeDtypeStruct((1,), f32), jax...  1.69 us

profile of v5, /device:TPU:1, one launch (start us, length us, event | category | flops | bytes accessed | tf_op | source)
XLA Modules:
  0.0 46.3 jit_solution(11581744027970992451)
XLA Ops:
  1.3 43.4 %contrast.1 = (f32[1,128]{1,0:T(1,128)}, f32[64,512]{1,0:T(8,128)}, f32[64,512]{1,0:T(8,128)}) custom-call(bf16[64,512]{1,0:T(8,128)(2,1)} %image_ref.1, bf16[64,512]{1,0:T(8,128)(2,1)} %text_ref.1, f32[1]{0:T(128)S(6)} %copy.6.scale_ref), custom_call_target="tpu_custom_call" | custom-call | flops 3221225472 | bytes 400000 | tf_op jit(solution)/shard_map/contrast/pallas_call | solution.py:446
  44.7 1.7 %write_out.1 = (f32[1]{0:T(128)}, f32[64,512]{1,0:T(8,128)}, f32[64,512]{1,0:T(8,128)}) custom-call(f32[1,128]{1,0:T(1,128)} %get-tuple-element.6.loss_in, f32[64,512]{1,0:T(8,128)} %get-tuple-element.7.img_in, f32[64,512]{1,0:T(8,128)} %get-tuple-element.8.txt_in), custom_call_target="tpu_custom_call" | custom-call | tf_op jit(solution)/shard_map/write_out/pallas_call | solution.py:495
